TPU v7x, 128 devices: a whole 4x4x4 slice. The times are simulated.
128 devices in a mesh: ex: 16 (over z, y), stk: 8 (over x, core).
Axes of the slice: x: 4, y: 4, z: 4, core: 2. Of those that a mesh axis runs over, the one named last changes fastest.
Arguments:
- embeddings: bfloat16 [4096, 4096], P(None, 'ex'), may hold values from -6 to 6
- sign_bits: int32 [16, 4096], P('stk'), may hold values from 0 to 1
- permutation: int32 [16, 4096], P('stk'), may hold values from 0 to 4095, each once within a row
- gaussian: float32 [16, 4096], P('stk'), may hold values from -6 to 6
- scaling: float32 [16, 4096], P('stk'), may hold values from 0.5 to 2
- phases: float32 [16, 4096], P('stk'), may hold values from -3.140625 to 3.140625
- solution: float32 [64, 16, 4096], P(None, 'stk', 'ex'), may hold values from -6 to 6
- residual: float32 [64, 16, 4096], P(None, 'stk', 'ex'), may hold values from -240 to 240
- direction: float32 [64, 16, 4096], P(None, 'stk', 'ex'), may hold values from -240 to 240
Outputs:
- solution_following: float32 [64, 16, 4096], P(None, 'stk', 'ex')
- residual_next: float32 [64, 16, 4096], P(None, 'stk', 'ex')
- direction_following: float32 [64, 16, 4096], P(None, 'stk', 'ex')
Inputs may be any that keep to these rules, and one draw needn't show every extreme that they name: `permutation`: each row holds every index of 0 to 4095 once.
All inputs are finite; a program needn't handle non-finite values.
Results may differ from a plain program's by a relative error of at most 0.0003.
Values sent between devices are 32-bit elements; how exact they have to be, the bound alone decides.
A program may use at most 128 MiB of HBM per device.

v0:
```python
from functools import partial
import math

import jax
import jax.numpy as jnp
from jax import lax
from jax.sharding import PartitionSpec as P

D = 4096
SIDE = 64


ridge = 0.25
epsilon = 1e-06


def parity_table(edge_size):
    counter = jnp.arange(edge_size, dtype=jnp.int32)
    common = jnp.zeros((edge_size, edge_size), jnp.int32)
    for bit_level in range(max(edge_size.bit_length() - 1, 1)):
        bit_vals = counter // 2**bit_level % 2
        common = common + bit_vals[:, None] * bit_vals[None, :]
    return (1 - 2 * (common % 2)).astype(jnp.float32)


def transform(field, walsh_hadamard_transform):
    edge_size = walsh_hadamard_transform.shape[0]
    columns = field.shape[1]
    blocked_layout = field.reshape(edge_size, edge_size, columns)
    blocked_layout = jnp.einsum(
        "ev,vtq->etq", walsh_hadamard_transform, blocked_layout, precision=lax.Precision.HIGHEST
    )
    blocked_layout = jnp.einsum(
        "aq,zqx->zax", walsh_hadamard_transform, blocked_layout, precision=lax.Precision.HIGHEST
    )
    return blocked_layout.reshape(edge_size * edge_size, columns)


def stack_panel(
    data, walsh_hadamard_transform, weight_norm, sign_row, perm_row, gauss_row, scale_row, phase_row
):
    signed = data * (2 * sign_row - 1).astype(jnp.float32)[:, None]
    spread_row_block = transform(signed, walsh_hadamard_transform)
    shuffled = jnp.take(spread_row_block, perm_row, axis=0) * gauss_row[:, None]
    angles = (
        scale_row[:, None] * transform(shuffled, walsh_hadamard_transform) / data.shape[0]
        + phase_row[:, None]
    )
    return weight_norm * jnp.cos(angles)


def target_sum(left, right):
    return jnp.sum(left * right, axis=(1, 2))


def local(
    embeddings, sign_bits, permutation, gaussian, scaling, phases, solution, residual, direction
):
    stack_count = sign_bits.shape[0]
    features_total = stack_count * lax.axis_size("stk") * D
    weight_norm = math.sqrt(2.0 / features_total)
    walsh_hadamard_transform = parity_table(SIDE)
    gathered = lax.all_gather(direction, "ex", axis=2, tiled=True)
    build = partial(
        stack_panel, embeddings.astype(jnp.float32), walsh_hadamard_transform, weight_norm
    )
    panel = jax.vmap(build)(sign_bits, permutation, gaussian, scaling, phases)
    partial_rows = jnp.einsum("tsj,sjn->tn", gathered, panel, precision=lax.Precision.HIGHEST)
    projected = lax.psum(partial_rows, "stk")
    partial_image = jnp.einsum("tn,sjn->tsj", projected, panel, precision=lax.Precision.HIGHEST)
    image_all = lax.psum(partial_image, "ex")
    slice_width = direction.shape[2]
    image_own = lax.dynamic_slice_in_dim(
        image_all, lax.axis_index("ex") * slice_width, slice_width, 2
    )
    applied = ridge * direction + image_own
    norm_old = lax.psum(target_sum(residual, residual), ("ex", "stk"))
    direction_curvature = lax.psum(target_sum(direction, applied), ("ex", "stk"))
    step_size = norm_old / direction_curvature
    residual_next = residual - step_size[:, None, None] * applied
    norm_new = lax.psum(target_sum(residual_next, residual_next), ("ex", "stk"))
    solution_following = solution + step_size[:, None, None] * direction
    conjugacy = norm_new / (norm_old + epsilon)
    direction_following = residual_next + conjugacy[:, None, None] * direction
    return (solution_following, residual_next, direction_following)


def solution(mesh):
    return jax.shard_map(
        local,
        mesh=mesh,
        in_specs=(
            P(None, "ex"),
            P("stk", None),
            P("stk", None),
            P("stk", None),
            P("stk", None),
            P("stk", None),
            P(None, "stk", "ex"),
            P(None, "stk", "ex"),
            P(None, "stk", "ex"),
        ),
        out_specs=(P(None, "stk", "ex"), P(None, "stk", "ex"), P(None, "stk", "ex")),
        check_vma=False,
    )
```

profile of v0, /device:TPU:1, one launch (start us, length us, event | category | flops | bytes accessed | tf_op | source)
XLA Modules:
  0.0 555.5 jit_solution(8264859775346908800)
XLA Ops:
  7.2 0.0 all-gather.2.cloned.1.call-start
  7.2 0.7 all-gather.2.cloned.1.call-update
  7.9 0.0 all-reduce.4.cloned.1.call-start
  8.0 4.1 convert.1
  12.1 0.8 add_convert_fusion
  12.8 0.1 mul.315
  13.0 2.8 broadcast_multiply_fusion
  15.8 12.7 %fusion.10 = f32[64,2,64,256]{3,0,2,1:T(8,128)S(1)} fusion(f32[2,64,64,256]{3,2,1,0:T(8,128)S(1)} %broadcast_multiply_fusion, s32[64]{0:T(128)S(1)} %get-tuple-element.14, s32[64]{0:T(128)S(1)} %get-tuple-element.15, s32[64]{0:T(128)S(1)} %get-tuple-element.16, s32[64]{0:T(128)S(1)} %get-tuple-element.17, s32[64]{0:T(128)S(1)} %get-tuple-element.18, ...), kind=kOutput, calls=%fused_computation.12 | convolution fusion | flops 1610715136 | bytes 16778752 | tf_op jit(solution)/shard_map/vmap(ev,vtq->etq)/dot_general | solution.py:30
  28.5 14.1 %fusion.12 = f32[2,64,64,256]{3,2,0,1:T(8,128)S(1)} fusion(f32[64,2,64,256]{3,0,2,1:T(8,128)S(1)} %fusion.10, s32[64]{0:T(128)S(1)} %get-tuple-element.14, s32[64]{0:T(128)S(1)} %get-tuple-element.15, s32[64]{0:T(128)S(1)} %get-tuple-element.16, s32[64]{0:T(128)S(1)} %get-tuple-element.17, s32[64]{0:T(128)S(1)} %get-tuple-element.18, ...), kind=kOutput, calls=%fused_computation.16 | convolution fusion | flops 1610715136 | bytes 16778752 | tf_op jit(solution)/shard_map/vmap(aq,zqx->zax)/dot_general | solution.py:33
  42.6 0.0 copy-start.2
  42.6 0.0 copy-start.6
  42.6 3.8 copy.22
  46.4 0.0 copy-done.2
  46.5 0.0 copy-done.6
  46.5 0.1 mul.318
  46.6 0.1 broadcast_in_dim.11
  46.7 130.6 %gather_fusion = f32[8192,256]{1,0:T(8,128)} fusion(f32[2,4096,256]{2,1,0:T(8,128)} %bitcast.43, s32[8192]{0:T(1024)S(1)} %bitcast.44), kind=kCustom, calls=%fused_computation | custom fusion | bytes 16842752 | tf_op jit(solution)/shard_map/vmap(jit(_take))/gather | solution.py:44
  177.4 6.9 %select_multiply_fusion = f32[2,64,64,256]{3,2,1,0:T(8,128)S(1)} fusion(f32[2,64,64,256]{3,2,1,0:T(8,128)} %bitcast.45, f32[2,64,64]{2,1,0:T(8,128)S(1)} %mul.318, pred[2,64,64]{2,1,0:T(8,128)(4,1)S(1)} %broadcast_in_dim.11), kind=kLoop, calls=%fused_computation.14 | loop fusion | flops 4194304 | bytes 16818176 | tf_op jit(solution)/shard_map/vmap()/mul | solution.py:44
  184.3 12.7 %fusion.6 = f32[64,2,64,256]{3,0,2,1:T(8,128)S(1)} fusion(f32[2,64,64,256]{3,2,1,0:T(8,128)S(1)} %select_multiply_fusion, s32[64]{0:T(128)S(1)} %get-tuple-element.14, s32[64]{0:T(128)S(1)} %get-tuple-element.15, s32[64]{0:T(128)S(1)} %get-tuple-element.16, s32[64]{0:T(128)S(1)} %get-tuple-element.17, s32[64]{0:T(128)S(1)} %get-tuple-element.18, ...), kind=kOutput, calls=%fused_computation.8 | convolution fusion | flops 1610715136 | bytes 16778752 | tf_op jit(solution)/shard_map/vmap(ev,vtq->etq)/dot_general | solution.py:30
  196.9 14.0 %fusion.15 = f32[2,64,64,256]{3,2,0,1:T(8,128)S(1)} fusion(f32[64,2,64,256]{3,0,2,1:T(8,128)S(1)} %fusion.6, s32[64]{0:T(128)S(1)} %get-tuple-element.14, s32[64]{0:T(128)S(1)} %get-tuple-element.15, s32[64]{0:T(128)S(1)} %get-tuple-element.16, s32[64]{0:T(128)S(1)} %get-tuple-element.17, s32[64]{0:T(128)S(1)} %get-tuple-element.18, ...), kind=kOutput, calls=%fused_computation.17 | convolution fusion | flops 1610715136 | bytes 16778752 | tf_op jit(solution)/shard_map/vmap(aq,zqx->zax)/dot_general | solution.py:33
  211.0 0.0 copy-start.4
  211.0 0.0 copy-start.5
  211.0 1.1 copy.23
  212.1 0.0 copy-done.4
  212.1 0.0 copy-done.5
  212.1 30.8 %fusion.3 = f32[2,4096,256]{2,1,0:T(8,128)} fusion(f32[2,64,64,256]{3,2,1,0:T(8,128)S(1)} %copy.23, f32[2,4096]{1,0:T(2,128)S(1)} %copy-done.4, f32[2,4096]{1,0:T(2,128)S(1)} %copy-done.5), kind=kLoop, calls=%fused_computation.5 | loop fusion | flops 8388608 | bytes 16842752 | tf_op jit(solution)/shard_map/vmap()/mul | solution.py:49
  242.9 0.0 all-gather.2.cloned.1.call-done
  243.0 10.2 %fusion.20 = f32[64,256]{1,0:T(8,128)} fusion(f32[2,4096,256]{2,1,0:T(8,128)} %fusion.3, f32[64,2,4096]{2,1,0:T(2,128)} %all-gather.2.cloned.1.call-done), kind=kOutput, calls=%fused_computation.20 | convolution fusion | flops 1610612736 | bytes 10551296 | tf_op jit(solution)/shard_map/tsj,sjn->tn/dot_general | solution.py:68
  253.2 0.0 copy-start.1
  253.2 0.0 copy-start
  253.2 0.0 all-reduce.4.cloned.1.call-update
  253.2 0.2 all-reduce.6.cloned.1.call-start
  253.4 59.6 %all-reduce.4.cloned.1.call-done = f32[64,256]{1,0:T(8,128)} async-done(((f32[64,256]{1,0:T(8,128)}), f32[64,256]{1,0:T(8,128)}) %all-reduce.4.cloned.1.call-update) | async-done | bytes 65552 | tf_op jit(solution)/shard_map/psum | solution.py:69
  313.0 12.7 %fusion.23 = f32[64,2,4096]{2,0,1:T(8,128)} fusion(f32[2,4096,256]{2,1,0:T(8,128)} %fusion.3, f32[64,256]{1,0:T(8,128)} %all-reduce.4.cloned.1.call-done), kind=kOutput, calls=%fused_computation.29 | convolution fusion | flops 1610612736 | bytes 10551296 | tf_op jit(solution)/shard_map/tn,sjn->tsj/dot_general | solution.py:70
  325.7 0.0 all-reduce.6.cloned.1.call-update
  325.8 0.0 copy-done.1
  325.8 0.6 multiply_reduce_fusion.2
  326.3 90.1 %all-reduce.6.cloned.1.call-done = f32[64,2,4096]{2,0,1:T(8,128)} async-done(((f32[64,2,4096]{2,0,1:T(8,128)}), f32[64,2,4096]{2,0,1:T(8,128)}) %all-reduce.6.cloned.1.call-update) | async-done | bytes 2097168 | tf_op jit(solution)/shard_map/psum | solution.py:71
  416.4 0.0 copy-done
  416.4 1.0 multiply_reduce_fusion.1
  417.4 65.3 %all-reduce = (f32[64]{0:T(128)S(1)}, f32[64]{0:T(128)S(1)}) all-reduce(f32[64]{0:T(128)S(1)} %multiply_reduce_fusion.2, f32[64]{0:T(128)S(1)} %multiply_reduce_fusion.1), channel_id=1, replica_groups=mesh['ex'=16,'stk'=8] {'ex','stk'}, use_global_device_ids=true, to_apply=%region_1.2 | all-reduce | flops 128 | bytes 1024 | tf_op jit(solution)/shard_map/psum | solution.py:77
  482.8 0.0 copy-done.3
  482.8 1.1 multiply_reduce_fusion
  483.9 62.6 %psum.39 = f32[64]{0:T(128)S(1)} all-reduce(f32[64]{0:T(128)S(1)} %get-tuple-element.11), channel_id=1, replica_groups=mesh['ex'=16,'stk'=8] {'ex','stk'}, use_global_device_ids=true, to_apply=%region_7.8 | all-reduce | flops 64 | bytes 512 | tf_op jit(solution)/shard_map/psum | solution.py:81
  546.4 0.8 copy.30
  547.2 0.1 multiply_add_fusion
  547.3 0.8 copy.31
  548.0 0.8 copy.29
  (9 shorter events, 0.1 us)
Async XLA Ops:
  7.2 235.8 %all-gather.2.cloned.1.call-start = ((), (), s32[]{:S(2)}) async-start(), calls=%async_computation | async-start | bytes 2228224 | tf_op jit(solution)/shard_map/all_gather | solution.py:63
  7.9 305.1 %all-reduce.4.cloned.1.call-start = ((), (), s32[]{:S(2)}) async-start(), calls=%async_computation.1 | async-start | bytes 131072 | tf_op jit(solution)/shard_map/psum | solution.py:69
  42.6 3.8 copy-start.2
  42.6 3.9 copy-start.6
  211.0 1.1 copy-start.4
  211.0 1.1 copy-start.5
  253.2 72.6 %copy-start.1 = (f32[64,2,256]{2,1,0:T(2,128)S(1)}, f32[64,2,256]{2,1,0:T(2,128)}, u32[]{:S(2)}) copy-start(f32[64,2,256]{2,1,0:T(2,128)} %param.16) | copy-start | bytes 393220
  253.2 163.2 %copy-start = (f32[64,2,256]{2,1,0:T(2,128)S(1)}, f32[64,2,256]{2,1,0:T(2,128)}, u32[]{:S(2)}) copy-start(f32[64,2,256]{2,1,0:T(2,128)} %param.17) | copy-start | bytes 393220
  253.2 229.6 %copy-start.3 = (f32[64,2,256]{2,1,0:T(2,128)S(1)}, f32[64,2,256]{2,1,0:T(2,128)}, u32[]{:S(2)}) copy-start(f32[64,2,256]{2,1,0:T(2,128)} %param.15) | copy-start | bytes 393220
  253.2 163.2 %all-reduce.6.cloned.1.call-start = ((), (), s32[]{:S(2)}) async-start(), calls=%async_computation.2 | async-start | bytes 4194304 | tf_op jit(solution)/shard_map/psum | solution.py:71
Sparse Core Ops, SparseCore 0:
  10.1 50.1 all-gather.1
  253.3 59.6 all-reduce.3
  325.9 90.4 all-reduce.5
where the time goes:
time: 566 us; the launch traced here: 556 us
  waiting for transfers between devices  150 us (27%)
  local copies, waits for them, and re-layouts  138 us (24%)
  blocking collectives  128 us (23%)
  matrix products  76.4 us (13%)
  other arithmetic  48.3 us (9%)
  between operations  14.1 us (2%)
    gather x1, local copies, waits for them, and re-layouts, stack_panel(): shuffled = jnp.take(spread_row_block, perm_row, axis=0) * gauss_row[:, None]  131 us
    psum x1, waiting for transfers between devices, local(): image_all = lax.psum(partial_image, 'ex')  90.1 us
    psum x1, blocking collectives, local(): norm_old = lax.psum(target_sum(residual, residual), ('ex', 'stk'))  65.3 us
    psum x1, blocking collectives, local(): norm_new = lax.psum(target_sum(residual_next, residual_next), ('ex', 'stk'))  62.6 us
    psum x1, waiting for transfers between devices, local(): projected = lax.psum(partial_rows, 'stk')  59.6 us
    mul x1, other arithmetic, stack_panel(): return weight_norm * jnp.cos(angles)  30.8 us
    dot_general x2, matrix products, transform(): jnp.einsum('aq,zqx->zax', walsh_hadamard_transform, blocked_layout, preci...  28.1 us
    dot_general x2, matrix products, transform(): jnp.einsum('ev,vtq->etq', walsh_hadamard_transform, blocked_layout, preci...  25.3 us
  transfers between devices with their start and end apart: 3, of which 2 were waited for; matrix products, arithmetic and copies ran while one was open for 42% of the time, Pallas kernels for 0%

commit v1 on v0

v1 whole, which is shorter than its diff:
```python
import functools
import math

import jax
import jax.numpy as jnp
from jax import lax
from jax.experimental import pallas as pl
from jax.experimental.pallas import tpu as pltpu
from jax.sharding import PartitionSpec as P

f32, bf16 = jnp.float32, jnp.bfloat16
MESH = pl.DeviceIdType.MESH

D = 4096
BLK = 256
NB = 16
NS = 8
T = 64
RIDGE = 0.25
EPSILON = 1e-06
TURN = 1.0 / (2.0 * math.pi)
NORM = math.sqrt(2.0 / (16 * D))
SINE = (6.283164044251588, -41.337142364570006, 81.34076867837481, -70.99343135659183)
COEF = tuple(c * NORM for c in SINE)


def hadamard():
    i = lax.broadcasted_iota(jnp.int32, (BLK, BLK), 0)
    j = lax.broadcasted_iota(jnp.int32, (BLK, BLK), 1)
    v = i & j
    v = v ^ (v >> 4)
    v = v ^ (v >> 2)
    v = v ^ (v >> 1)
    return (1 - 2 * (v & 1)).astype(f32)


def butterfly(values):
    v = list(values)
    h = 1
    while h < len(v):
        for i in range(0, len(v), 2 * h):
            for k in range(i, i + h):
                v[k], v[k + h] = v[k] + v[k + h], v[k] - v[k + h]
        h *= 2
    return v


def split(x):
    hi = x.astype(bf16)
    return hi, (x - hi.astype(f32)).astype(bf16)


def dot(a, b):
    return jnp.dot(a, b, preferred_element_type=f32)


def dot_t(a, b):
    return lax.dot_general(a, b, (((1,), (1,)), ((), ())), preferred_element_type=f32)


def row_sums(x):
    ones = jnp.ones((8, x.shape[1]), f32)
    return lax.dot_general(
        ones, x, (((1,), (1,)), ((), ())), precision=lax.Precision.HIGHEST, preferred_element_type=f32
    )


def column(row):
    wide = jnp.concatenate([row, row], axis=1)
    return jnp.transpose(wide)[:T, 0:1]


def columns_of_parameters(gauss, scale, phase, col):
    for b in range(D // 128):
        at = slice(b * 128, (b + 1) * 128)
        block = jnp.concatenate(
            [
                gauss[:, at],
                scale[:, at] * (TURN / D),
                phase[:, at] * TURN,
                jnp.zeros((2, 128), f32),
            ],
            axis=0,
        )
        col[at, :] = jnp.transpose(block)


def spread_blocks(s, sign, emb, h, y):
    def body(a, _):
        o = pl.multiple_of(a * BLK, BLK)
        signs = (2 * sign[s : s + 1, pl.ds(o, BLK)] - 1).astype(f32)
        y[pl.ds(o, BLK), :] = dot((h * signs).astype(bf16), emb[pl.ds(o, BLK), :])
        return 0

    lax.fori_loop(0, NB, body, 0, unroll=4)


def spread_across(y, sp):
    def body(r, _):
        o = pl.multiple_of(r * 8, 8)
        for half in range(2):
            lanes = slice(half * 128, (half + 1) * 128)
            v = butterfly([y[pl.ds(a * BLK + o, 8), lanes] for a in range(NB)])
            for a in range(NB):
                sp[half, pl.ds(a * BLK + o, 8), :] = v[a]
        return 0

    lax.fori_loop(0, BLK // 8, body, 0)


def permute(perm, sp, y):
    groups = 8

    def body(jb, _):
        o = pl.multiple_of(jb * 8 * groups, 8 * groups)
        for q in range(groups):
            at = pl.multiple_of(o + q * 8, 8)
            rows = [y.at[pl.ds(at, 8), half * 128 : (half + 1) * 128] for half in range(2)]
            for k in range(8):
                idx = perm[o + q * 8 + k]
                for half in range(2):
                    rows[half][k : k + 1, :] = sp[half, pl.ds(idx, 1), :]
        return 0

    lax.fori_loop(0, D // (8 * groups), body, 0)


def mix_across(s, y, col, z):
    def body(r, _):
        o = pl.multiple_of(r * 16, 16)
        gauss = [jnp.broadcast_to(col[pl.ds(a * BLK + o, 16), s : s + 1], (16, 128)) for a in range(NB)]
        for half in range(2):
            lanes = slice(half * 128, (half + 1) * 128)
            v = butterfly([y[pl.ds(a * BLK + o, 16), lanes] * gauss[a] for a in range(NB)])
            for a in range(NB):
                hi, lo = split(v[a])
                z[a, pl.ds(o, 16), lanes] = hi
                z[a, pl.ds(BLK + o, 16), lanes] = lo
        return 0

    lax.fori_loop(0, BLK // 16, body, 0)


def cosine(turns):
    x = 0.25 - jnp.abs(turns - jnp.round(turns))
    u = x * x
    p = COEF[3]
    for c in COEF[2::-1]:
        p = p * u + c
    return p * x


def features(s, z, h2, col, fh, fl):
    def body(a, _):
        o = pl.multiple_of(a * BLK, BLK)
        scale = col[pl.ds(o, BLK), 2 + s : 3 + s]
        phase = col[pl.ds(o, BLK), 4 + s : 5 + s]
        hi, lo = split(cosine(dot(h2, z[a]) * scale + phase))
        fh[s, a] = hi
        fl[s, a] = lo
        return 0

    lax.fori_loop(0, NB, body, 0, unroll=2)


def kernel(
    emb, sign, perm_hbm, gauss, scale, phase, sol, res, dire,
    sol_out, res_out, dir_out,
    perm0, perm1, y, sp, z, fh, fl, col,
    dall, stat, stat2, pacc, precv, pown, pfull, isend, irecv, pp, nn, nn2,
    perm_sem, d_send, d_recv, st_send, st_recv, st2_send, st2_recv,
    p1_send, p1_recv, p2_send, p2_recv, i_send, i_recv, pp_send, pp_recv,
    n1_send, n1_recv, n2_send, n2_recv,
):
    ex = lax.axis_index("ex")
    st = lax.axis_index("stk")
    ez, ey = ex // 4, ex % 4

    def ex_to(k):
        return ((ez + k // 4) % 4) * 4 + (ey + k % 4) % 4

    def ex_from(k):
        return ((ez + 4 - k // 4) % 4) * 4 + (ey + 4 - k % 4) % 4

    def st_to(k):
        return (st + k) % NS

    def st_from(k):
        return (st + NS - k) % NS

    def to_ex(k, src, dst, send, recv):
        return pltpu.make_async_remote_copy(
            src_ref=src, dst_ref=dst, send_sem=send.at[k], recv_sem=recv.at[k],
            device_id=(ex_to(k), st), device_id_type=MESH,
        )

    def to_st(k, src, dst, send, recv):
        return pltpu.make_async_remote_copy(
            src_ref=src, dst_ref=dst, send_sem=send.at[k], recv_sem=recv.at[k],
            device_id=(ex, st_to(k)), device_id_type=MESH,
        )

    def each(n, f):
        def body(k, _):
            f(k)
            return 0

        lax.fori_loop(1, n, body, 0)

    barrier = pltpu.get_barrier_semaphore()
    each(NB, lambda k: pl.semaphore_signal(barrier, inc=1, device_id=(ex_to(k), st), device_id_type=MESH))
    each(NS, lambda k: pl.semaphore_signal(barrier, inc=1, device_id=(ex, st_to(k)), device_id_type=MESH))
    perms = [perm0, perm1]
    perm_copies = [pltpu.make_async_copy(perm_hbm.at[s], perms[s], perm_sem.at[s]) for s in range(2)]
    for c in perm_copies:
        c.start()

    for s in range(2):
        dall[ex, s] = dire[:, s, :]
    r2 = row_sums(jnp.concatenate([jnp.square(res[:, s, :]) for s in range(2)], axis=1))
    d2 = row_sums(jnp.concatenate([jnp.square(dire[:, s, :]) for s in range(2)], axis=1))
    stat[0] = jnp.concatenate([r2, d2], axis=1)

    h = hadamard()
    hb = h.astype(bf16)
    h2 = jnp.concatenate([hb, hb], axis=1)
    columns_of_parameters(gauss, scale, phase, col)
    spread_blocks(0, sign, emb, h, y)

    pl.semaphore_wait(barrier, NB - 1 + NS - 1)

    def d_copy(k):
        return to_ex(k, dall.at[ex], dall.at[ex], d_send, d_recv)

    def st_copy(k):
        return to_ex(k, stat.at[0], stat.at[k], st_send, st_recv)

    each(NB, lambda k: st_copy(k).start())
    each(NB, lambda k: d_copy(k).start())

    spread_across(y, sp)
    perm_copies[0].wait()
    permute(perms[0], sp, y)
    mix_across(0, y, col, z)
    features(0, z, h2, col, fh, fl)

    each(NB, lambda k: st_copy(k).wait())
    stat2[0] = jnp.sum(stat[...], axis=0)

    def st2_copy(k):
        return to_st(k, stat2.at[0], stat2.at[k], st2_send, st2_recv)

    each(NS, lambda k: st2_copy(k).start())

    spread_blocks(1, sign, emb, h, y)
    spread_across(y, sp)
    perm_copies[1].wait()
    permute(perms[1], sp, y)
    mix_across(1, y, col, z)
    features(1, z, h2, col, fh, fl)

    each(NS, lambda k: st2_copy(k).wait())
    totals = jnp.sum(stat2[...], axis=0)
    norm_old, d_norm = totals[:, :T], totals[:, T:]

    def project(e):
        for s in range(2):
            hi, lo = split(dall[e, s])
            both = dot(jnp.concatenate([hi, lo], axis=0), fh[s, e])
            pacc[...] += both[:T] + both[T:] + dot(hi, fl[s, e])

    pacc[...] = jnp.zeros_like(pacc)
    project(ex)

    def arrived(k):
        d_copy(k).wait_recv()
        project(ex_from(k))

    each(NB, arrived)

    def rows(i):
        return pl.ds(pl.multiple_of(i * 8, 8), 8)

    def p1_copy(k):
        return to_st(k, pacc.at[rows(st_to(k))], precv.at[k], p1_send, p1_recv)

    each(NS, lambda k: p1_copy(k).start())
    precv[0] = pacc[rows(st), :]
    each(NS, lambda k: p1_copy(k).wait_recv())
    pown[...] = jnp.sum(precv[...], axis=0)

    def p2_copy(k):
        return to_st(k, pown, pfull.at[rows(st)], p2_send, p2_recv)

    each(NS, lambda k: p2_copy(k).start())
    pfull[rows(st), :] = pown[...]

    def p2_arrived(k):
        pltpu.make_async_remote_copy(
            src_ref=pown, dst_ref=pfull.at[rows(st_from(k))], send_sem=p2_send.at[k], recv_sem=p2_recv.at[k],
            device_id=(ex, st_to(k)), device_id_type=MESH,
        ).wait_recv()

    each(NS, p2_arrived)

    projected = pfull[...]
    p_hi, p_lo = split(projected)
    p_both = jnp.concatenate([p_hi, p_lo], axis=0)

    def image(e):
        for s in range(2):
            both = dot_t(p_both, fh[s, e])
            isend[e, s] = both[:T] + both[T:] + dot_t(p_hi, fl[s, e])

    def i_copy(k):
        return to_ex(k, isend.at[ex_to(k)], irecv.at[k], i_send, i_recv)

    def image_out(k):
        image(ex_to(k))
        i_copy(k).start()

    each(NB, image_out)
    image(ex)
    irecv[0] = isend[ex]

    pp_row = row_sums(jnp.square(projected))
    pp[0] = jnp.concatenate([pp_row, pp_row], axis=1)

    def pp_copy(k):
        return to_ex(k, pp.at[0], pp.at[k], pp_send, pp_recv)

    each(NB, lambda k: pp_copy(k).start())
    each(NB, lambda k: pp_copy(k).wait())
    p_norm = jnp.sum(pp[...], axis=0)[:, :T]
    step = column(norm_old / (RIDGE * d_norm + p_norm))

    for s in range(2):
        sol_out[:, s, :] = sol[:, s, :] + step * dire[:, s, :]

    each(NB, lambda k: i_copy(k).wait_recv())
    nexts = []
    for s in range(2):
        applied = RIDGE * dire[:, s, :] + jnp.sum(irecv[:, s], axis=0)
        nexts.append(res[:, s, :] - step * applied)
        res_out[:, s, :] = nexts[s]
    n_row = row_sums(jnp.concatenate([jnp.square(v) for v in nexts], axis=1))
    nn[0] = jnp.concatenate([n_row, n_row], axis=1)

    def n1_copy(k):
        return to_ex(k, nn.at[0], nn.at[k], n1_send, n1_recv)

    each(NB, lambda k: n1_copy(k).start())
    each(NB, lambda k: n1_copy(k).wait())
    nn2[0] = jnp.sum(nn[...], axis=0)

    def n2_copy(k):
        return to_st(k, nn2.at[0], nn2.at[k], n2_send, n2_recv)

    each(NS, lambda k: n2_copy(k).start())
    each(NS, lambda k: n2_copy(k).wait())
    norm_new = jnp.sum(nn2[...], axis=0)[:, :T]
    conjugacy = column(norm_new / (norm_old + EPSILON))
    for s in range(2):
        dir_out[:, s, :] = nexts[s] + conjugacy * dire[:, s, :]

    each(NB, lambda k: d_copy(k).wait_send())
    each(NB, lambda k: i_copy(k).wait_send())
    each(NS, lambda k: p1_copy(k).wait_send())
    each(NS, lambda k: p2_copy(k).wait_send())


def local(embeddings, sign_bits, permutation, gaussian, scaling, phases, solution, residual, direction):
    vmem = pl.BlockSpec(memory_space=pltpu.VMEM)
    shape = jax.ShapeDtypeStruct(direction.shape, f32)
    dma = pltpu.SemaphoreType.DMA
    return pl.pallas_call(
        kernel,
        out_shape=[shape] * 3,
        in_specs=[vmem, vmem, pl.BlockSpec(memory_space=pl.ANY)] + [vmem] * 6,
        out_specs=[vmem] * 3,
        scratch_shapes=[
            pltpu.SMEM((D,), jnp.int32),
            pltpu.SMEM((D,), jnp.int32),
            pltpu.VMEM((D, BLK), f32),
            pltpu.VMEM((2, D, 128), f32),
            pltpu.VMEM((NB, 2 * BLK, BLK), bf16),
            pltpu.VMEM((2, NB, BLK, BLK), bf16),
            pltpu.VMEM((2, NB, BLK, BLK), bf16),
            pltpu.VMEM((D, 8), f32),
            pltpu.VMEM((NB, 2, T, BLK), f32),
            pltpu.VMEM((NB, 8, 128), f32),
            pltpu.VMEM((NS, 8, 128), f32),
            pltpu.VMEM((T, BLK), f32),
            pltpu.VMEM((NS, 8, BLK), f32),
            pltpu.VMEM((8, BLK), f32),
            pltpu.VMEM((T, BLK), f32),
            pltpu.VMEM((NB, 2, T, BLK), f32),
            pltpu.VMEM((NB, 2, T, BLK), f32),
            pltpu.VMEM((NB, 8, 128), f32),
            pltpu.VMEM((NB, 8, 128), f32),
            pltpu.VMEM((NS, 8, 128), f32),
            dma((2,)),
            dma((NB,)), dma((NB,)), dma((NB,)), dma((NB,)), dma((NS,)), dma((NS,)),
            dma((NS,)), dma((NS,)), dma((NS,)), dma((NS,)), dma((NB,)), dma((NB,)), dma((NB,)), dma((NB,)),
            dma((NB,)), dma((NB,)), dma((NS,)), dma((NS,)),
        ],
        compiler_params=pltpu.CompilerParams(
            collective_id=0, has_side_effects=True, vmem_limit_bytes=52 * 2**20
        ),
    )(embeddings, sign_bits, permutation, gaussian, scaling, phases, solution, residual, direction)


def solution(mesh):
    rows, stacks, blocks = P(None, "ex"), P("stk", None), P(None, "stk", "ex")
    return jax.shard_map(
        local,
        mesh=mesh,
        in_specs=(rows, stacks, stacks, stacks, stacks, stacks, blocks, blocks, blocks),
        out_specs=(blocks, blocks, blocks),
        check_vma=False,
    )
```

time: 566 us -> 107 us (0.19); the launches traced: 556 us -> 107 us
  waiting for transfers between devices: 150 us -> 0 us
  local copies, waits for them, and re-layouts: 138 us -> 8.46 us
  blocking collectives: 128 us -> 0 us
  Pallas kernels: 0 us -> 97.8 us
  matrix products: 76.4 us -> 0 us
  other arithmetic: 48.3 us -> 0 us
  between operations: 14.1 us -> 0.66 us
    psum x2 -> x0, waiting for transfers between devices: 150 us -> none  [the longest x1 90.1 us: local(): image_all = lax.psum(partial_image, 'ex')]
    gather x1 -> x0, local copies, waits for them, and re-layouts: 131 us -> none  [stack_panel(): shuffled = jnp.take(spread_row_block, perm_row, axis=0) * gauss_row[:, None]]
    psum x2 -> x0, blocking collectives: 128 us -> none  [the longest x1 65.3 us: local(): norm_old = lax.psum(target_sum(residual, residual), ('ex', 'stk'))]
    pallas_call x0 -> x1, Pallas kernels: none -> 97.8 us  [local(): pl.pallas_call(kernel, out_shape=[shape] * 3, in_specs=[vmem, vmem, pl.Bl...]
    dot_general x6 -> x0, matrix products: 76.4 us -> none  [the longest x2 28.1 us: transform(): jnp.einsum('aq,zqx->zax', walsh_hadamard_transform, blocked_layout, preci...]
    mul x4 -> x0, other arithmetic: 44.6 us -> none  [the longest x1 30.8 us: stack_panel(): return weight_norm * jnp.cos(angles)]
    unnamed x18 -> x19, local copies, waits for them, and re-layouts: 2.32 us -> 8.46 us
  transfers between devices with their start and end apart: 3 -> 0, of which waited for: 2 -> 0; matrix products, arithmetic and copies ran while one was open for 42% -> 0% of each run, Pallas kernels for 0% -> 0%
where the time goes in v1:
time: 107 us
  Pallas kernels  97.8 us (91%)
  local copies, waits for them, and re-layouts  8.46 us (8%)
    pallas_call x1, Pallas kernels, local(): pl.pallas_call(kernel, out_shape=[shape] * 3, in_specs=[vmem, vmem, pl.Bl...  97.8 us
    unnamed x19, local copies, waits for them, and re-layouts  8.46 us

profile of v1, /device:TPU:1, one launch (start us, length us, event | category | flops | bytes accessed | tf_op | source)
XLA Modules:
  0.0 106.9 jit_solution(11500785461655103226)
XLA Ops:
  0.6 0.0 copy-start
  0.6 0.9 copy-done
  1.5 0.0 copy-start.1
  1.5 0.9 copy-done.1
  2.4 0.0 copy-start.2
  2.4 0.9 copy-done.2
  3.3 0.0 copy-start.3
  3.4 0.8 copy-done.3
  4.1 0.0 copy-start.4
  4.1 0.8 copy-done.4
  4.9 0.0 copy-start.5
  4.9 0.8 copy-done.5
  5.6 0.0 copy-start.6
  5.6 0.8 copy-done.6
  6.4 0.0 copy-start.7
  6.4 0.8 copy-done.7
  7.1 97.8 %shard_map.112 = (f32[64,2,256]{2,1,0:T(2,128)S(1)}, f32[64,2,256]{2,1,0:T(2,128)S(1)}, f32[64,2,256]{2,1,0:T(2,128)S(1)}) custom-call(bf16[4096,256]{1,0:T(8,128)(2,1)} %emb.1, s32[2,4096]{1,0:T(2,128)S(1)} %copy-done.3, s32[2,4096]{1,0:T(2,128)S(1)} %copy-done.4, f32[2,4096]{1,0:T(2,128)S(1)} %copy-done.5, f32[2,4096]{1,0:T(2,128)S(1)} %copy-done.6, ...), custom_call_target="tpu_custom_call" | custom-call | tf_op jit(solution)/shard_map/pallas_call | solution.py:376
  105.0 0.7 copy.15
  105.6 0.7 copy.16
  106.3 0.7 copy.17
Async XLA Ops:
  0.6 0.9 copy-start
  1.5 0.9 copy-start.1
  2.4 0.9 copy-start.2
  3.3 0.8 copy-start.3
  4.1 0.8 copy-start.4
  4.9 0.8 copy-start.5
  5.6 0.8 copy-start.6
  6.4 0.8 copy-start.7

commit v2 on v1

v2 whole, which is shorter than its diff:
```python
import functools
import math

import jax
import jax.numpy as jnp
from jax import lax
from jax.experimental import pallas as pl
from jax.experimental.pallas import tpu as pltpu
from jax.sharding import PartitionSpec as P

f32, bf16 = jnp.float32, jnp.bfloat16
MESH = pl.DeviceIdType.MESH

D = 4096
BLK = 256
NB = 16
NS = 8
T = 64
RIDGE = 0.25
EPSILON = 1e-06
TURN = 1.0 / (2.0 * math.pi)
NORM = math.sqrt(2.0 / (16 * D))
SINE = (6.283164044251588, -41.337142364570006, 81.34076867837481, -70.99343135659183)
COEF = tuple(c * NORM for c in SINE)


def hadamard():
    i = lax.broadcasted_iota(jnp.int32, (BLK, BLK), 0)
    j = lax.broadcasted_iota(jnp.int32, (BLK, BLK), 1)
    v = i & j
    v = v ^ (v >> 4)
    v = v ^ (v >> 2)
    v = v ^ (v >> 1)
    return (1 - 2 * (v & 1)).astype(f32)


def butterfly(values):
    v = list(values)
    h = 1
    while h < len(v):
        for i in range(0, len(v), 2 * h):
            for k in range(i, i + h):
                v[k], v[k + h] = v[k] + v[k + h], v[k] - v[k + h]
        h *= 2
    return v


def split(x):
    hi = x.astype(bf16)
    return hi, (x - hi.astype(f32)).astype(bf16)


def dot(a, b):
    return jnp.dot(a, b, preferred_element_type=f32)


def dot_t(a, b):
    return lax.dot_general(a, b, (((1,), (1,)), ((), ())), preferred_element_type=f32)


def row_sums(x):
    ones = jnp.ones((8, x.shape[1]), f32)
    return lax.dot_general(
        ones, x, (((1,), (1,)), ((), ())), precision=lax.Precision.HIGHEST, preferred_element_type=f32
    )


def column(row):
    wide = jnp.concatenate([row, row], axis=1)
    return jnp.transpose(wide)[:T, 0:1]


def columns_of_parameters(gauss, scale, phase, col):
    for b in range(D // 128):
        at = slice(b * 128, (b + 1) * 128)
        block = jnp.concatenate(
            [
                gauss[:, at],
                scale[:, at] * (TURN / D),
                phase[:, at] * TURN,
                jnp.zeros((2, 128), f32),
            ],
            axis=0,
        )
        col[at, :] = jnp.transpose(block)


def spread_blocks(s, sign, emb, h, y):
    def body(a, _):
        o = pl.multiple_of(a * BLK, BLK)
        signs = (2 * sign[s : s + 1, pl.ds(o, BLK)] - 1).astype(f32)
        y[pl.ds(o, BLK), :] = dot((h * signs).astype(bf16), emb[pl.ds(o, BLK), :])
        return 0

    lax.fori_loop(0, NB, body, 0, unroll=4)


def spread_across(y, sp):
    def body(r, _):
        o = pl.multiple_of(r * 8, 8)
        for half in range(2):
            lanes = slice(half * 128, (half + 1) * 128)
            v = butterfly([y[pl.ds(a * BLK + o, 8), lanes] for a in range(NB)])
            for a in range(NB):
                sp[half, pl.ds(a * BLK + o, 8), :] = v[a]
        return 0

    lax.fori_loop(0, BLK // 8, body, 0)


def permute(perm, sp, y):
    groups = 8
    sub = lax.broadcasted_iota(jnp.int32, (8, 128), 0)

    def body(jb, _):
        o = pl.multiple_of(jb * 8 * groups, 8 * groups)
        for q in range(groups):
            at = pl.multiple_of(o + q * 8, 8)
            idx = [perm[o + q * 8 + k] for k in range(8)]
            for half in range(2):
                rows = [jnp.broadcast_to(sp[half, pl.ds(i, 1), :], (8, 128)) for i in idx]
                acc = rows[0]
                for k in range(1, 8):
                    acc = jnp.where(sub == k, rows[k], acc)
                y[pl.ds(at, 8), half * 128 : (half + 1) * 128] = acc
        return 0

    lax.fori_loop(0, D // (8 * groups), body, 0)


def mix_across(s, y, col, z):
    def body(r, _):
        o = pl.multiple_of(r * 16, 16)
        gauss = [jnp.broadcast_to(col[pl.ds(a * BLK + o, 16), s : s + 1], (16, 128)) for a in range(NB)]
        for half in range(2):
            lanes = slice(half * 128, (half + 1) * 128)
            v = butterfly([y[pl.ds(a * BLK + o, 16), lanes] * gauss[a] for a in range(NB)])
            for a in range(NB):
                hi, lo = split(v[a])
                z[a, pl.ds(o, 16), lanes] = hi
                z[a, pl.ds(BLK + o, 16), lanes] = lo
        return 0

    lax.fori_loop(0, BLK // 16, body, 0)


def cosine(turns):
    x = 0.25 - jnp.abs(turns - jnp.round(turns))
    u = x * x
    p = COEF[3]
    for c in COEF[2::-1]:
        p = p * u + c
    return p * x


def features(s, z, h2, col, fh, fl, also=None):
    def body(a, _):
        o = pl.multiple_of(a * BLK, BLK)
        scale = col[pl.ds(o, BLK), 2 + s : 3 + s]
        phase = col[pl.ds(o, BLK), 4 + s : 5 + s]
        hi, lo = split(cosine(dot(h2, z[a]) * scale + phase))
        fh[s, a] = hi
        fl[s, a] = lo
        if also is not None:
            also(a, hi, lo)
        return 0

    lax.fori_loop(0, NB, body, 0, unroll=2)


def kernel(
    emb_h, sign_h, perm_h, gauss_h, scale_h, phase_h, res_h, dire_h,
    applied_out, step_out, conj_out,
    emb, sign, gauss, scale, phase, res, dire, perm0, perm1, in_sem, out_sem,
    y, sp, z, fh, fl, col,
    da, db, stat, stat2, pacc, psib, pchip, px, sa, sb, ra1, rb1, sa2, sb2, ra2, rb2, app, wide, pp, pp2, nn, nn2,
    d1_send, d1_recv, d2_send, d2_recv, st_send, st_recv, st2_send, st2_recv,
    p1_send, p1_recv, p2_send, p2_recv, i1_send, i1_recv, i2_send, i2_recv,
    pp_send, pp_recv, pp2_send, pp2_recv, n1_send, n1_recv, n2_send, n2_recv,
):
    ex = lax.axis_index("ex")
    st = lax.axis_index("stk")
    ez, ey = ex // 4, ex % 4

    def ring(i, k):
        return (i + k) % 4

    def ex_dev(dz, dy):
        return (ring(ez, dz) * 4 + ring(ey, dy), st)

    def st_dev(k):
        return (ex, (st + k) % NS)

    sibling = (ex, st + 1 - 2 * (st % 2))

    def remote(dev, src, dst, send, recv):
        return pltpu.make_async_remote_copy(
            src_ref=src, dst_ref=dst, send_sem=send, recv_sem=recv, device_id=dev, device_id_type=MESH
        )

    def each(n, f, first=1):
        def body(k, _):
            f(k)
            return 0

        lax.fori_loop(first, n, body, 0)

    def ex_k(k):
        return ex_dev(k // 4, k % 4)

    inputs = [
        pltpu.make_async_copy(src, dst, in_sem.at[i])
        for i, (src, dst) in enumerate(
            [
                (dire_h, dire), (res_h, res), (sign_h, sign), (emb_h, emb), (gauss_h, gauss),
                (scale_h, scale), (phase_h, phase), (perm_h.at[0], perm0), (perm_h.at[1], perm1),
            ]
        )
    ]
    for c in inputs:
        c.start()
    barrier = pltpu.get_barrier_semaphore()
    each(NB, lambda k: pl.semaphore_signal(barrier, inc=1, device_id=ex_k(k), device_id_type=MESH))
    each(NS, lambda k: pl.semaphore_signal(barrier, inc=1, device_id=st_dev(k), device_id_type=MESH))

    h = hadamard()
    hb = h.astype(bf16)
    h2 = jnp.concatenate([hb, hb], axis=1)

    inputs[0].wait()
    inputs[1].wait()
    own_a, own_b = ex, ey * 4 + ez
    da[own_a] = dire[:, 0, :]
    db[own_b] = dire[:, 1, :]

    pl.semaphore_wait(barrier, NB - 1 + NS - 1)

    def d1_copy(a, k):
        if a:
            return remote(ex_dev(0, k), da.at[own_a], da.at[own_a], d1_send.at[0, k], d1_recv.at[0, k])
        return remote(ex_dev(k, 0), db.at[own_b], db.at[own_b], d1_send.at[1, k], d1_recv.at[1, k])

    def d2_copy(a, k):
        four_a, four_b = da.at[pl.ds(ez * 4, 4)], db.at[pl.ds(ey * 4, 4)]
        if a:
            return remote(ex_dev(k, 0), four_a, four_a, d2_send.at[0, k], d2_recv.at[0, k])
        return remote(ex_dev(0, k), four_b, four_b, d2_send.at[1, k], d2_recv.at[1, k])

    def both(f):
        def go(k):
            f(True, k)
            f(False, k)

        each(4, go)

    both(lambda a, k: d1_copy(a, k).start())

    def st_copy(k):
        return remote(ex_k(k), stat.at[0], stat.at[k], st_send.at[k], st_recv.at[k])

    r2 = row_sums(jnp.concatenate([jnp.square(res[:, s, :]) for s in range(2)], axis=1))
    d2 = row_sums(jnp.concatenate([jnp.square(dire[:, s, :]) for s in range(2)], axis=1))
    stat[0] = jnp.concatenate([r2, d2], axis=1)
    each(NB, lambda k: st_copy(k).start())

    inputs[2].wait()
    inputs[3].wait()
    spread_blocks(0, sign, emb, h, y)
    spread_across(y, sp)
    for i in (4, 5, 6, 7, 8):
        inputs[i].wait()
    columns_of_parameters(gauss, scale, phase, col)
    permute(perm0, sp, y)

    both(lambda a, k: d1_copy(a, k).wait_recv())
    both(lambda a, k: d2_copy(a, k).start())

    mix_across(0, y, col, z)
    features(0, z, h2, col, fh, fl)

    each(NB, lambda k: st_copy(k).wait())
    stat2[0] = jnp.sum(stat[...], axis=0)

    def st2_copy(k):
        return remote(st_dev(k), stat2.at[0], stat2.at[k], st2_send.at[k], st2_recv.at[k])

    each(NS, lambda k: st2_copy(k).start())

    spread_blocks(1, sign, emb, h, y)
    spread_across(y, sp)
    permute(perm1, sp, y)
    mix_across(1, y, col, z)

    each(NS, lambda k: st2_copy(k).wait())
    totals = jnp.sum(stat2[...], axis=0)
    norm_old, d_norm = totals[:, :T], totals[:, T:]
    both(lambda a, k: d2_copy(a, k).wait_recv())

    def project(a, hi1, lo1):
        hi, lo = split(da[a])
        both0 = dot(jnp.concatenate([hi, lo], axis=0), fh[0, a])
        both0_lo = dot(hi, fl[0, a])
        hi, lo = split(db[(a % 4) * 4 + a // 4])
        both1 = dot(jnp.concatenate([hi, lo], axis=0), hi1)
        pacc[...] += (both0[:T] + both1[:T]) + (both0[T:] + both1[T:] + both0_lo + dot(hi, lo1))

    pacc[...] = jnp.zeros_like(pacc)
    features(1, z, h2, col, fh, fl, project)

    def p1_copy():
        return remote(sibling, pacc, psib, p1_send, p1_recv)

    p1_copy().start()
    p1_copy().wait_recv()
    pchip[...] = pacc[...] + psib[...]

    def p2_copy(k):
        return remote(st_dev(2 * k), pchip, px.at[k], p2_send.at[k], p2_recv.at[k])

    each(4, lambda k: p2_copy(k).start())
    px[0] = pchip[...]
    each(4, lambda k: p2_copy(k).wait_recv())
    projected = (px[0] + px[1]) + (px[2] + px[3])
    p_hi, p_lo = split(projected)
    p_both = jnp.concatenate([p_hi, p_lo], axis=0)

    pp_row = row_sums(jnp.square(projected))
    pp[0] = jnp.concatenate([pp_row, pp_row], axis=1)

    def pp_copy(k):
        return remote(ex_dev(0, k), pp.at[0], pp.at[k], pp_send.at[k], pp_recv.at[k])

    def pp2_copy(k):
        return remote(ex_dev(k, 0), pp2.at[0], pp2.at[k], pp2_send.at[k], pp2_recv.at[k])

    each(4, lambda k: pp_copy(k).start())

    def image(s, e):
        big = dot_t(p_both, fh[s, e])
        return big[:T] + big[T:] + dot_t(p_hi, fl[s, e])

    def i1_copy(a, near, far):
        if a:
            return remote(
                ex_dev(0, near), sa.at[near, far], ra1.at[near, far], i1_send.at[0, near, far], i1_recv.at[0, near, far]
            )
        return remote(
            ex_dev(near, 0), sb.at[near, far], rb1.at[near, far], i1_send.at[1, near, far], i1_recv.at[1, near, far]
        )

    def image_out(i):
        far, near = (i // 4 + 1) % 4, (i + 1) % 4
        sa[near, far] = image(0, ring(ez, far) * 4 + ring(ey, near))
        sb[near, far] = image(1, ring(ez, near) * 4 + ring(ey, far))

        @pl.when(near > 0)
        def _():
            i1_copy(True, near, far).start()
            i1_copy(False, near, far).start()

    each(16, image_out, 0)

    each(4, lambda k: pp_copy(k).wait())
    pp2[0] = jnp.sum(pp[...], axis=0)
    each(4, lambda k: pp2_copy(k).start())

    def i2_copy(a, k):
        if a:
            return remote(ex_dev(k, 0), sa2.at[k], ra2.at[k], i2_send.at[0, k], i2_recv.at[0, k])
        return remote(ex_dev(0, k), sb2.at[k], rb2.at[k], i2_send.at[1, k], i2_recv.at[1, k])

    def forward(far):
        for a, src, got, out in ((True, sa, ra1, sa2), (False, sb, rb1, sb2)):
            each(4, lambda near: i1_copy(a, near, far).wait_recv())
            out[far] = (src[0, far] + got[1, far]) + (got[2, far] + got[3, far])

    def forward_out(far):
        forward(far)
        i2_copy(True, far).start()
        i2_copy(False, far).start()

    each(4, forward_out)

    each(4, lambda k: pp2_copy(k).wait())
    p_norm = jnp.sum(pp2[...], axis=0)[:, :T]
    step = column(norm_old / (RIDGE * d_norm + p_norm))
    wide[0] = jnp.broadcast_to(step, (T, 128))
    step_copy = pltpu.make_async_copy(wide.at[0], step_out, out_sem.at[0])
    step_copy.start()

    forward(0)
    both(lambda a, k: i2_copy(a, k).wait_recv())
    squares = []
    for s, own, got in ((0, sa2, ra2), (1, sb2, rb2)):
        applied = RIDGE * dire[:, s, :] + ((own[0] + got[1]) + (got[2] + got[3]))
        app[:, s, :] = applied
        squares.append(jnp.square(res[:, s, :] - step * applied))
    app_copy = pltpu.make_async_copy(app, applied_out, out_sem.at[1])
    app_copy.start()
    n_row = row_sums(jnp.concatenate(squares, axis=1))
    nn[0] = jnp.concatenate([n_row, n_row], axis=1)

    def n1_copy(k):
        return remote(ex_k(k), nn.at[0], nn.at[k], n1_send.at[k], n1_recv.at[k])

    each(NB, lambda k: n1_copy(k).start())
    each(NB, lambda k: n1_copy(k).wait())
    nn2[0] = jnp.sum(nn[...], axis=0)

    def n2_copy(k):
        return remote(st_dev(k), nn2.at[0], nn2.at[k], n2_send.at[k], n2_recv.at[k])

    each(NS, lambda k: n2_copy(k).start())
    both(lambda a, k: d1_copy(a, k).wait_send())
    both(lambda a, k: d2_copy(a, k).wait_send())
    p1_copy().wait_send()
    each(4, lambda k: p2_copy(k).wait_send())

    def i1_sent(i):
        near, far = i // 4 + 1, i % 4
        i1_copy(True, near, far).wait_send()
        i1_copy(False, near, far).wait_send()

    each(12, i1_sent, 0)
    both(lambda a, k: i2_copy(a, k).wait_send())
    step_copy.wait()
    app_copy.wait()
    each(NS, lambda k: n2_copy(k).wait())
    norm_new = jnp.sum(nn2[...], axis=0)[:, :T]
    wide[1] = jnp.broadcast_to(column(norm_new / (norm_old + EPSILON)), (T, 128))
    conj_copy = pltpu.make_async_copy(wide.at[1], conj_out, out_sem.at[2])
    conj_copy.start()
    conj_copy.wait()


def local(embeddings, sign_bits, permutation, gaussian, scaling, phases, solution, residual, direction):
    hbm = pl.BlockSpec(memory_space=pltpu.HBM)
    dma = pltpu.SemaphoreType.DMA
    vmem = pltpu.VMEM
    block, tile = (T, BLK), (8, 128)
    applied, step, conjugacy = pl.pallas_call(
        kernel,
        out_shape=[
            jax.ShapeDtypeStruct(direction.shape, f32),
            jax.ShapeDtypeStruct((T, 128), f32),
            jax.ShapeDtypeStruct((T, 128), f32),
        ],
        in_specs=[hbm] * 8,
        out_specs=[hbm] * 3,
        scratch_shapes=[
            vmem((D, BLK), bf16),
            vmem((2, D), jnp.int32),
            vmem((2, D), f32),
            vmem((2, D), f32),
            vmem((2, D), f32),
            vmem(direction.shape, f32),
            vmem(direction.shape, f32),
            pltpu.SMEM((D,), jnp.int32),
            pltpu.SMEM((D,), jnp.int32),
            dma((9,)),
            dma((3,)),
            vmem((D, BLK), f32),
            vmem((2, D, 128), f32),
            vmem((NB, 2 * BLK, BLK), bf16),
            vmem((2, NB, BLK, BLK), bf16),
            vmem((2, NB, BLK, BLK), bf16),
            vmem((D, 8), f32),
            vmem((NB,) + block, f32),
            vmem((NB,) + block, f32),
            vmem((NB,) + tile, f32),
            vmem((NS,) + tile, f32),
            vmem(block, f32),
            vmem(block, f32),
            vmem(block, f32),
            vmem((4,) + block, f32),
            vmem((4, 4) + block, f32),
            vmem((4, 4) + block, f32),
            vmem((4, 4) + block, f32),
            vmem((4, 4) + block, f32),
            vmem((4,) + block, f32),
            vmem((4,) + block, f32),
            vmem((4,) + block, f32),
            vmem((4,) + block, f32),
            vmem(direction.shape, f32),
            vmem((2, T, 128), f32),
            vmem((4,) + tile, f32),
            vmem((4,) + tile, f32),
            vmem((NB,) + tile, f32),
            vmem((NS,) + tile, f32),
            dma((2, 4)), dma((2, 4)), dma((2, 4)), dma((2, 4)),
            dma((NB,)), dma((NB,)), dma((NS,)), dma((NS,)),
            dma, dma, dma((4,)), dma((4,)),
            dma((2, 4, 4)), dma((2, 4, 4)), dma((2, 4)), dma((2, 4)),
            dma((4,)), dma((4,)), dma((4,)), dma((4,)),
            dma((NB,)), dma((NB,)), dma((NS,)), dma((NS,)),
        ],
        compiler_params=pltpu.CompilerParams(
            collective_id=0, has_side_effects=True, vmem_limit_bytes=60 * 2**20
        ),
    )(embeddings, sign_bits, permutation, gaussian, scaling, phases, residual, direction)
    step = step[:, :1, None]
    conjugacy = conjugacy[:, :1, None]
    residual_next = residual - step * applied
    return solution + step * direction, residual_next, residual_next + conjugacy * direction


def solution(mesh):
    rows, stacks, blocks = P(None, "ex"), P("stk", None), P(None, "stk", "ex")
    return jax.shard_map(
        local,
        mesh=mesh,
        in_specs=(rows, stacks, stacks, stacks, stacks, stacks, blocks, blocks, blocks),
        out_specs=(blocks, blocks, blocks),
        check_vma=False,
    )
```

time: 107 us -> 78.5 us (0.73)
  Pallas kernels: 97.8 us -> 74.8 us
  local copies, waits for them, and re-layouts: 8.46 us -> 0.89 us
  other arithmetic: 0 us -> 1.87 us
    pallas_call x1, Pallas kernels: 97.8 us -> 74.8 us  [local(): pl.pallas_call(kernel, out_shape=[jax.ShapeDtypeStruct(direction.shape, f...]
    unnamed x19 -> x6, local copies, waits for them, and re-layouts: 8.46 us -> 0.01 us
    add x0 -> x1, other arithmetic: none -> 1.87 us  [local(): residual_next + conjugacy * direction]
where the time goes in v2:
time: 78.5 us; the launch traced here: 78.3 us
  Pallas kernels  74.8 us (95%)
  other arithmetic  1.87 us (2%)
  local copies, waits for them, and re-layouts  0.89 us (1%)
    pallas_call x1, Pallas kernels, local(): pl.pallas_call(kernel, out_shape=[jax.ShapeDtypeStruct(direction.shape, f...  74.8 us
    add x1, other arithmetic, local(): residual_next + conjugacy * direction  1.87 us

profile of v2, /device:TPU:1, one launch (start us, length us, event | category | flops | bytes accessed | tf_op | source)
XLA Modules:
  0.0 78.3 jit_solution(11983266613612490541)
XLA Ops:
  0.6 0.0 copy-start
  0.6 0.0 copy-start.1
  0.7 0.0 copy-start.2
  0.7 74.8 %shard_map.112 = (f32[64,2,256]{2,1,0:T(2,128)}, f32[64,128]{1,0:T(8,128)}, f32[64,128]{1,0:T(8,128)}) custom-call(bf16[4096,256]{1,0:T(8,128)(2,1)} %emb_h.1, s32[2,4096]{1,0:T(2,128)} %sign_h.1, s32[2,4096]{1,0:T(2,128)} %perm_h.1, f32[2,4096]{1,0:T(2,128)} %gauss_h.1, f32[2,4096]{1,0:T(2,128)} %scale_h.1, f32[2,4096]{1,0:T(2,128)} %phase_h.1, ...), custom_call_target="tpu_custom_call" | custom-call | tf_op jit(solution)/shard_map/pallas_call | solution.py:441
  75.5 0.9 %slice_reduce_fusion = (f32[64]{0:T(128)S(1)}, f32[64]{0:T(128)S(1)}) fusion(f32[64,128]{1,0:T(8,128)} %get-tuple-element.8, f32[64,128]{1,0:T(8,128)} %get-tuple-element.6), kind=kLoop, calls=%fused_computation.3 | loop fusion | bytes 1024 | tf_op jit(solution)/shard_map/slice | solution.py:502
  76.3 0.0 copy-done
  76.4 0.0 copy-done.1
  76.4 0.0 copy-done.2
  76.4 1.9 %multiply_add_fusion = (f32[64,2,256]{2,1,0:T(2,128)}, f32[64,2,256]{2,1,0:T(2,128)}, f32[64,2,256]{2,1,0:T(2,128)}) fusion(f32[64,2,256]{2,1,0:T(2,128)S(1)} %copy-done, f32[64]{0:T(128)S(1)} %get-tuple-element.12, f32[64,2,256]{2,1,0:T(2,128)S(1)} %copy-done.1, f32[64,2,256]{2,1,0:T(2,128)} %get-tuple-element.7, f32[64]{0:T(128)S(1)} %get-tuple-element.13, ...), kind=kLoop, calls=%fused_computation | loop fusion | flops 196608 | bytes 918016 | tf_op jit(solution)/shard_map/add | solution.py:504
Async XLA Ops:
  0.6 75.7 %copy-start = (f32[64,2,256]{2,1,0:T(2,128)S(1)}, f32[64,2,256]{2,1,0:T(2,128)}, u32[]{:S(2)}) copy-start(f32[64,2,256]{2,1,0:T(2,128)} %dire_h.1) | copy-start | bytes 393220
  0.6 75.7 %copy-start.1 = (f32[64,2,256]{2,1,0:T(2,128)S(1)}, f32[64,2,256]{2,1,0:T(2,128)}, u32[]{:S(2)}) copy-start(f32[64,2,256]{2,1,0:T(2,128)} %res_h.1) | copy-start | bytes 393220
  0.7 75.7 %copy-start.2 = (f32[64,2,256]{2,1,0:T(2,128)S(1)}, f32[64,2,256]{2,1,0:T(2,128)}, u32[]{:S(2)}) copy-start(f32[64,2,256]{2,1,0:T(2,128)} %param.15) | copy-start | bytes 393220

commit v3 on v2

--- a/solution.py
+++ b/solution.py
@@ -85,63 +85,62 @@
         col[at, :] = jnp.transpose(block)
 
 
-def spread_blocks(s, sign, emb, h, y):
-    def body(a, _):
-        o = pl.multiple_of(a * BLK, BLK)
-        signs = (2 * sign[s : s + 1, pl.ds(o, BLK)] - 1).astype(f32)
-        y[pl.ds(o, BLK), :] = dot((h * signs).astype(bf16), emb[pl.ds(o, BLK), :])
-        return 0
-
-    lax.fori_loop(0, NB, body, 0, unroll=4)
-
-
-def spread_across(y, sp):
-    def body(r, _):
-        o = pl.multiple_of(r * 8, 8)
+def spread_block(s, a, sign, emb, h, y):
+    o = pl.multiple_of(a * BLK, BLK)
+    signs = (2 * sign[s : s + 1, pl.ds(o, BLK)] - 1).astype(f32)
+    y[pl.ds(o, BLK), :] = dot((h * signs).astype(bf16), emb[pl.ds(o, BLK), :])
+
+
+def spread_across(r, y, sp):
+    o = pl.multiple_of(r * 8, 8)
+    for half in range(2):
+        lanes = slice(half * 128, (half + 1) * 128)
+        v = butterfly([y[pl.ds(a * BLK + o, 8), lanes] for a in range(NB)])
+        for a in range(NB):
+            sp[half, pl.ds(a * BLK + o, 8), :] = v[a]
+
+
+def permute(base, rows, perm, sp, y, sub):
+    for q in range(rows // 8):
+        at = pl.multiple_of(base + q * 8, 8)
+        idx = [perm[base + q * 8 + k] for k in range(8)]
         for half in range(2):
             lanes = slice(half * 128, (half + 1) * 128)
-            v = butterfly([y[pl.ds(a * BLK + o, 8), lanes] for a in range(NB)])
-            for a in range(NB):
-                sp[half, pl.ds(a * BLK + o, 8), :] = v[a]
+            if sub is None:
+                out = y.at[pl.ds(at, 8), lanes]
+                for k in range(8):
+                    out[k : k + 1, :] = sp[half, pl.ds(idx[k], 1), :]
+            else:
+                row = [jnp.broadcast_to(sp[half, pl.ds(i, 1), :], (8, 128)) for i in idx]
+                acc = row[0]
+                for k in range(1, 8):
+                    acc = jnp.where(sub == k, row[k], acc)
+                y[pl.ds(at, 8), lanes] = acc
+
+
+def mix_across(r, y, bc, z):
+    o = pl.multiple_of(r * 16, 16)
+    for half in range(2):
+        lanes = slice(half * 128, (half + 1) * 128)
+        v = butterfly(
+            [
+                y[pl.ds(a * BLK + o, 16), lanes]
+                * bc[0, pl.ds(a * BLK + o, 16), :]
+                for a in range(NB)
+            ]
+        )
+        for a in range(NB):
+            hi, lo = split(v[a])
+            z[a, pl.ds(o, 16), lanes] = hi
+            z[a, pl.ds(BLK + o, 16), lanes] = lo
+
+
+def loop(n, f, unroll=1):
+    def body(i, _):
+        f(i)
         return 0
 
-    lax.fori_loop(0, BLK // 8, body, 0)
-
-
-def permute(perm, sp, y):
-    groups = 8
-    sub = lax.broadcasted_iota(jnp.int32, (8, 128), 0)
-
-    def body(jb, _):
-        o = pl.multiple_of(jb * 8 * groups, 8 * groups)
-        for q in range(groups):
-            at = pl.multiple_of(o + q * 8, 8)
-            idx = [perm[o + q * 8 + k] for k in range(8)]
-            for half in range(2):
-                rows = [jnp.broadcast_to(sp[half, pl.ds(i, 1), :], (8, 128)) for i in idx]
-                acc = rows[0]
-                for k in range(1, 8):
-                    acc = jnp.where(sub == k, rows[k], acc)
-                y[pl.ds(at, 8), half * 128 : (half + 1) * 128] = acc
-        return 0
-
-    lax.fori_loop(0, D // (8 * groups), body, 0)
-
-
-def mix_across(s, y, col, z):
-    def body(r, _):
-        o = pl.multiple_of(r * 16, 16)
-        gauss = [jnp.broadcast_to(col[pl.ds(a * BLK + o, 16), s : s + 1], (16, 128)) for a in range(NB)]
-        for half in range(2):
-            lanes = slice(half * 128, (half + 1) * 128)
-            v = butterfly([y[pl.ds(a * BLK + o, 16), lanes] * gauss[a] for a in range(NB)])
-            for a in range(NB):
-                hi, lo = split(v[a])
-                z[a, pl.ds(o, 16), lanes] = hi
-                z[a, pl.ds(BLK + o, 16), lanes] = lo
-        return 0
-
-    lax.fori_loop(0, BLK // 16, body, 0)
+    lax.fori_loop(0, n, body, 0, unroll=unroll)
 
 
 def cosine(turns):
@@ -153,26 +152,31 @@
     return p * x
 
 
-def features(s, z, h2, col, fh, fl, also=None):
-    def body(a, _):
-        o = pl.multiple_of(a * BLK, BLK)
-        scale = col[pl.ds(o, BLK), 2 + s : 3 + s]
-        phase = col[pl.ds(o, BLK), 4 + s : 5 + s]
-        hi, lo = split(cosine(dot(h2, z[a]) * scale + phase))
-        fh[s, a] = hi
-        fl[s, a] = lo
+def spread_parameters(s, a, col, bc):
+    at = pl.ds(pl.multiple_of(a * BLK, BLK), BLK)
+    for v in range(3):
+        bc[v, at, :] = jnp.broadcast_to(col[at, 2 * v + s : 2 * v + s + 1], (BLK, 128))
+
+
+def features(s, a, ang, bc, fh, fl, also=None):
+    o = pl.multiple_of(a * BLK, BLK)
+    for c in range(8):
+        rows = slice(c * 32, (c + 1) * 32)
+        at = pl.ds(o + c * 32, 32)
+        for half in range(2):
+            lanes = slice(half * 128, (half + 1) * 128)
+            hi, lo = split(cosine(ang[rows, lanes] * bc[1, at, :] + bc[2, at, :]))
+            fh[s, a, rows, lanes] = hi
+            fl[s, a, rows, lanes] = lo
         if also is not None:
-            also(a, hi, lo)
-        return 0
-
-    lax.fori_loop(0, NB, body, 0, unroll=2)
+            also(c)
 
 
 def kernel(
     emb_h, sign_h, perm_h, gauss_h, scale_h, phase_h, res_h, dire_h,
     applied_out, step_out, conj_out,
     emb, sign, gauss, scale, phase, res, dire, perm0, perm1, in_sem, out_sem,
-    y, sp, z, fh, fl, col,
+    y, sp, y1, sp1, z, fh, fl, col, bc0, bc1, ang0, ang1,
     da, db, stat, stat2, pacc, psib, pchip, px, sa, sb, ra1, rb1, sa2, sb2, ra2, rb2, app, wide, pp, pp2, nn, nn2,
     d1_send, d1_recv, d2_send, d2_recv, st_send, st_recv, st2_send, st2_recv,
     p1_send, p1_recv, p2_send, p2_recv, i1_send, i1_recv, i2_send, i2_recv,
@@ -233,6 +237,10 @@
     da[own_a] = dire[:, 0, :]
     db[own_b] = dire[:, 1, :]
 
+    inputs[2].wait()
+    inputs[3].wait()
+    loop(NB, lambda a: spread_block(0, a, sign, emb, h, y), 4)
+    loop(32, lambda r: spread_across(r, y, sp), 2)
     pl.semaphore_wait(barrier, NB - 1 + NS - 1)
 
     def d1_copy(a, k):
@@ -263,20 +271,48 @@
     stat[0] = jnp.concatenate([r2, d2], axis=1)
     each(NB, lambda k: st_copy(k).start())
 
-    inputs[2].wait()
-    inputs[3].wait()
-    spread_blocks(0, sign, emb, h, y)
-    spread_across(y, sp)
     for i in (4, 5, 6, 7, 8):
         inputs[i].wait()
     columns_of_parameters(gauss, scale, phase, col)
-    permute(perm0, sp, y)
+    sub = lax.broadcasted_iota(jnp.int32, (8, 128), 0)
+
+    def permute_spread(i):
+        for q in range(2):
+            spread_block(1, 2 * i + q, sign, emb, h, y1)
+            spread_parameters(0, 2 * i + q, col, bc0)
+            permute(pl.multiple_of(i * 256 + q * 128, 128), 128, perm0, sp, y, sub)
+
+    def permute_spread_across(i):
+        for q in range(4):
+            spread_across(4 * i + q, y1, sp1)
+            if q < 2:
+                spread_parameters(1, 2 * i + q, col, bc1)
+            permute(pl.multiple_of(D // 2 + i * 256 + q * 64, 64), 64, perm0, sp, y, sub)
+
+    loop(8, permute_spread)
+    loop(8, permute_spread_across)
 
     both(lambda a, k: d1_copy(a, k).wait_recv())
     both(lambda a, k: d2_copy(a, k).start())
 
-    mix_across(0, y, col, z)
-    features(0, z, h2, col, fh, fl)
+    def mix_permute(i):
+        mix_across(i, y, bc0, z)
+        permute(pl.multiple_of(i * 64, 64), 64, perm1, sp1, y1, None)
+
+    def features_permute(j):
+        for q in range(2):
+            i = 2 * j + q
+
+            def part(c):
+                n = (256 - 64) // 8
+                permute(pl.multiple_of(16 * 64 + i * (256 - 64) + c * n, 8), n, perm1, sp1, y1, None)
+
+            features(0, i, (ang0, ang1)[q], bc0, fh, fl, part)
+            (ang1, ang0)[q][...] = dot(h2, z[(i + 1) % NB])
+
+    loop(NB, mix_permute)
+    ang0[...] = dot(h2, z[0])
+    loop(NB // 2, features_permute)
 
     each(NB, lambda k: st_copy(k).wait())
     stat2[0] = jnp.sum(stat[...], axis=0)
@@ -286,26 +322,31 @@
 
     each(NS, lambda k: st2_copy(k).start())
 
-    spread_blocks(1, sign, emb, h, y)
-    spread_across(y, sp)
-    permute(perm1, sp, y)
-    mix_across(1, y, col, z)
+    loop(NB, lambda i: mix_across(i, y1, bc1, z))
 
     each(NS, lambda k: st2_copy(k).wait())
     totals = jnp.sum(stat2[...], axis=0)
     norm_old, d_norm = totals[:, :T], totals[:, T:]
     both(lambda a, k: d2_copy(a, k).wait_recv())
 
-    def project(a, hi1, lo1):
-        hi, lo = split(da[a])
-        both0 = dot(jnp.concatenate([hi, lo], axis=0), fh[0, a])
-        both0_lo = dot(hi, fl[0, a])
-        hi, lo = split(db[(a % 4) * 4 + a // 4])
-        both1 = dot(jnp.concatenate([hi, lo], axis=0), hi1)
-        pacc[...] += (both0[:T] + both1[:T]) + (both0[T:] + both1[T:] + both0_lo + dot(hi, lo1))
+    def project(a):
+        part = 0.0
+        for s, block in ((0, da[a]), (1, db[(a % 4) * 4 + a // 4])):
+            hi, lo = split(block)
+            big = dot(jnp.concatenate([hi, lo], axis=0), fh[s, a])
+            part += big[:T] + (big[T:] + dot(hi, fl[s, a]))
+        pacc[...] += part
+
+    def features_project(j):
+        for q in range(2):
+            i = 2 * j + q
+            features(1, i, (ang0, ang1)[q], bc1, fh, fl)
+            (ang1, ang0)[q][...] = dot(h2, z[(i + 1) % NB])
+            project(i)
 
     pacc[...] = jnp.zeros_like(pacc)
-    features(1, z, h2, col, fh, fl, project)
+    ang0[...] = dot(h2, z[0])
+    loop(NB // 2, features_project)
 
     def p1_copy():
         return remote(sibling, pacc, psib, p1_send, p1_recv)
@@ -461,10 +502,16 @@
             dma((3,)),
             vmem((D, BLK), f32),
             vmem((2, D, 128), f32),
+            vmem((D, BLK), f32),
+            vmem((2, D, 128), f32),
             vmem((NB, 2 * BLK, BLK), bf16),
             vmem((2, NB, BLK, BLK), bf16),
             vmem((2, NB, BLK, BLK), bf16),
             vmem((D, 8), f32),
+            vmem((3, D, 128), f32),
+            vmem((3, D, 128), f32),
+            vmem((BLK, BLK), f32),
+            vmem((BLK, BLK), f32),
             vmem((NB,) + block, f32),
             vmem((NB,) + block, f32),
             vmem((NB,) + tile, f32),

time: 78.5 us -> 77.9 us (level)
  no operation moved by 1% of the time
where the time goes in v3:
time: 77.9 us; the launch traced here: 77.6 us
  Pallas kernels  74.2 us (95%)
  other arithmetic  1.87 us (2%)
  local copies, waits for them, and re-layouts  0.89 us (1%)
    pallas_call x1, Pallas kernels, local(): pl.pallas_call(kernel, out_shape=[jax.ShapeDtypeStruct(direction.shape, f...  74.2 us
    add x1, other arithmetic, local(): residual_next + conjugacy * direction  1.87 us

profile of v3, /device:TPU:1, one launch (start us, length us, event | category | flops | bytes accessed | tf_op | source)
XLA Modules:
  0.0 77.6 jit_solution(5154932560808245962)
XLA Ops:
  0.6 0.0 copy-start
  0.6 0.0 copy-start.1
  0.7 0.0 copy-start.2
  0.7 74.2 %shard_map.112 = (f32[64,2,256]{2,1,0:T(2,128)}, f32[64,128]{1,0:T(8,128)}, f32[64,128]{1,0:T(8,128)}) custom-call(bf16[4096,256]{1,0:T(8,128)(2,1)} %emb_h.1, s32[2,4096]{1,0:T(2,128)} %sign_h.1, s32[2,4096]{1,0:T(2,128)} %perm_h.1, f32[2,4096]{1,0:T(2,128)} %gauss_h.1, f32[2,4096]{1,0:T(2,128)} %scale_h.1, f32[2,4096]{1,0:T(2,128)} %phase_h.1, ...), custom_call_target="tpu_custom_call" | custom-call | tf_op jit(solution)/shard_map/pallas_call | solution.py:482
  74.9 0.9 %slice_reduce_fusion = (f32[64]{0:T(128)S(1)}, f32[64]{0:T(128)S(1)}) fusion(f32[64,128]{1,0:T(8,128)} %get-tuple-element.8, f32[64,128]{1,0:T(8,128)} %get-tuple-element.6), kind=kLoop, calls=%fused_computation.3 | loop fusion | bytes 1024 | tf_op jit(solution)/shard_map/slice | solution.py:549
  75.7 0.0 copy-done
  75.8 0.0 copy-done.1
  75.8 0.0 copy-done.2
  75.8 1.9 %multiply_add_fusion = (f32[64,2,256]{2,1,0:T(2,128)}, f32[64,2,256]{2,1,0:T(2,128)}, f32[64,2,256]{2,1,0:T(2,128)}) fusion(f32[64,2,256]{2,1,0:T(2,128)S(1)} %copy-done, f32[64]{0:T(128)S(1)} %get-tuple-element.12, f32[64,2,256]{2,1,0:T(2,128)S(1)} %copy-done.1, f32[64,2,256]{2,1,0:T(2,128)} %get-tuple-element.7, f32[64]{0:T(128)S(1)} %get-tuple-element.13, ...), kind=kLoop, calls=%fused_computation | loop fusion | flops 196608 | bytes 918016 | tf_op jit(solution)/shard_map/add | solution.py:551
Async XLA Ops:
  0.6 75.1 %copy-start = (f32[64,2,256]{2,1,0:T(2,128)S(1)}, f32[64,2,256]{2,1,0:T(2,128)}, u32[]{:S(2)}) copy-start(f32[64,2,256]{2,1,0:T(2,128)} %dire_h.1) | copy-start | bytes 393220
  0.6 75.1 %copy-start.1 = (f32[64,2,256]{2,1,0:T(2,128)S(1)}, f32[64,2,256]{2,1,0:T(2,128)}, u32[]{:S(2)}) copy-start(f32[64,2,256]{2,1,0:T(2,128)} %res_h.1) | copy-start | bytes 393220
  0.7 75.1 %copy-start.2 = (f32[64,2,256]{2,1,0:T(2,128)S(1)}, f32[64,2,256]{2,1,0:T(2,128)}, u32[]{:S(2)}) copy-start(f32[64,2,256]{2,1,0:T(2,128)} %param.15) | copy-start | bytes 393220

commit v4 on v3

--- a/solution.py
+++ b/solution.py
@@ -97,35 +97,22 @@
         lanes = slice(half * 128, (half + 1) * 128)
         v = butterfly([y[pl.ds(a * BLK + o, 8), lanes] for a in range(NB)])
         for a in range(NB):
-            sp[half, pl.ds(a * BLK + o, 8), :] = v[a]
-
-
-def permute(base, rows, perm, sp, y, sub):
-    for q in range(rows // 8):
-        at = pl.multiple_of(base + q * 8, 8)
-        idx = [perm[base + q * 8 + k] for k in range(8)]
-        for half in range(2):
-            lanes = slice(half * 128, (half + 1) * 128)
-            if sub is None:
-                out = y.at[pl.ds(at, 8), lanes]
-                for k in range(8):
-                    out[k : k + 1, :] = sp[half, pl.ds(idx[k], 1), :]
-            else:
-                row = [jnp.broadcast_to(sp[half, pl.ds(i, 1), :], (8, 128)) for i in idx]
-                acc = row[0]
-                for k in range(1, 8):
-                    acc = jnp.where(sub == k, row[k], acc)
-                y[pl.ds(at, 8), lanes] = acc
-
-
-def mix_across(r, y, bc, z):
+            sp[pl.ds(2 * (a * BLK + o) + half, 8, stride=2), :] = v[a]
+
+
+def permute(base, rows, perm, sp, yg):
+    out = yg.at[pl.ds(pl.multiple_of(2 * base, 2 * 8), 2 * rows)]
+    for k in range(rows):
+        out[2 * k : 2 * k + 2, :] = sp[pl.ds(perm[base + k], 2), :]
+
+
+def mix_across(r, yg, bc, z):
     o = pl.multiple_of(r * 16, 16)
     for half in range(2):
         lanes = slice(half * 128, (half + 1) * 128)
         v = butterfly(
             [
-                y[pl.ds(a * BLK + o, 16), lanes]
-                * bc[0, pl.ds(a * BLK + o, 16), :]
+                yg[pl.ds(2 * (a * BLK + o) + half, 16, stride=2), :] * bc[0, pl.ds(a * BLK + o, 16), :]
                 for a in range(NB)
             ]
         )
@@ -175,10 +162,10 @@
 def kernel(
     emb_h, sign_h, perm_h, gauss_h, scale_h, phase_h, res_h, dire_h,
     applied_out, step_out, conj_out,
-    emb, sign, gauss, scale, phase, res, dire, perm0, perm1, in_sem, out_sem,
-    y, sp, y1, sp1, z, fh, fl, col, bc0, bc1, ang0, ang1,
-    da, db, stat, stat2, pacc, psib, pchip, px, sa, sb, ra1, rb1, sa2, sb2, ra2, rb2, app, wide, pp, pp2, nn, nn2,
-    d1_send, d1_recv, d2_send, d2_recv, st_send, st_recv, st2_send, st2_recv,
+    emb, sign, gauss, scale, phase, res, dire, pv, pv2, perm0, perm1, in_sem, perm_sem, out_sem,
+    y, sp, yg, sp1, yg1, z, fh, fl, col, bc0, bc1, ang0, ang1,
+    da, db, pacc, psib, pchip, px, sa, sb, ra1, rb1, sa2, sb2, ra2, rb2, app, wide, pp, pp2, nn, nn2,
+    d1_send, d1_recv, d2_send, d2_recv,
     p1_send, p1_recv, p2_send, p2_recv, i1_send, i1_recv, i2_send, i2_recv,
     pp_send, pp_recv, pp2_send, pp2_recv, n1_send, n1_recv, n2_send, n2_recv,
 ):
@@ -217,7 +204,7 @@
         for i, (src, dst) in enumerate(
             [
                 (dire_h, dire), (res_h, res), (sign_h, sign), (emb_h, emb), (gauss_h, gauss),
-                (scale_h, scale), (phase_h, phase), (perm_h.at[0], perm0), (perm_h.at[1], perm1),
+                (scale_h, scale), (phase_h, phase), (perm_h, pv),
             ]
         )
     ]
@@ -237,6 +224,13 @@
     da[own_a] = dire[:, 0, :]
     db[own_b] = dire[:, 1, :]
 
+    inputs[7].wait()
+    pv2[...] = 2 * pv[...]
+    perm_copies = [
+        pltpu.make_async_copy(pv2.at[s], p, perm_sem.at[s]) for s, p in enumerate((perm0, perm1))
+    ]
+    for c in perm_copies:
+        c.start()
     inputs[2].wait()
     inputs[3].wait()
     loop(NB, lambda a: spread_block(0, a, sign, emb, h, y), 4)
@@ -263,31 +257,29 @@
 
     both(lambda a, k: d1_copy(a, k).start())
 
-    def st_copy(k):
-        return remote(ex_k(k), stat.at[0], stat.at[k], st_send.at[k], st_recv.at[k])
-
     r2 = row_sums(jnp.concatenate([jnp.square(res[:, s, :]) for s in range(2)], axis=1))
     d2 = row_sums(jnp.concatenate([jnp.square(dire[:, s, :]) for s in range(2)], axis=1))
-    stat[0] = jnp.concatenate([r2, d2], axis=1)
-    each(NB, lambda k: st_copy(k).start())
-
-    for i in (4, 5, 6, 7, 8):
+    pacc[...] = jnp.zeros_like(pacc)
+    pacc[T:, :128] = jnp.concatenate([r2, d2], axis=1)
+
+    for i in (4, 5, 6):
         inputs[i].wait()
+    for c in perm_copies:
+        c.wait()
     columns_of_parameters(gauss, scale, phase, col)
-    sub = lax.broadcasted_iota(jnp.int32, (8, 128), 0)
 
     def permute_spread(i):
+        permute(pl.multiple_of(i * 256, 256), 256, perm0, sp, yg)
         for q in range(2):
-            spread_block(1, 2 * i + q, sign, emb, h, y1)
+            spread_block(1, 2 * i + q, sign, emb, h, y)
             spread_parameters(0, 2 * i + q, col, bc0)
-            permute(pl.multiple_of(i * 256 + q * 128, 128), 128, perm0, sp, y, sub)
 
     def permute_spread_across(i):
+        permute(pl.multiple_of(D // 2 + i * 256, 256), 256, perm0, sp, yg)
         for q in range(4):
-            spread_across(4 * i + q, y1, sp1)
-            if q < 2:
-                spread_parameters(1, 2 * i + q, col, bc1)
-            permute(pl.multiple_of(D // 2 + i * 256 + q * 64, 64), 64, perm0, sp, y, sub)
+            spread_across(4 * i + q, y, sp1)
+        for q in range(2):
+            spread_parameters(1, 2 * i + q, col, bc1)
 
     loop(8, permute_spread)
     loop(8, permute_spread_across)
@@ -296,37 +288,22 @@
     both(lambda a, k: d2_copy(a, k).start())
 
     def mix_permute(i):
-        mix_across(i, y, bc0, z)
-        permute(pl.multiple_of(i * 64, 64), 64, perm1, sp1, y1, None)
+        mix_across(i, yg, bc0, z)
+        permute(pl.multiple_of(i * 64, 64), 64, perm1, sp1, yg1)
 
     def features_permute(j):
         for q in range(2):
             i = 2 * j + q
-
-            def part(c):
-                n = (256 - 64) // 8
-                permute(pl.multiple_of(16 * 64 + i * (256 - 64) + c * n, 8), n, perm1, sp1, y1, None)
-
-            features(0, i, (ang0, ang1)[q], bc0, fh, fl, part)
+            features(0, i, (ang0, ang1)[q], bc0, fh, fl)
+            permute(pl.multiple_of(16 * 64 + i * 192, 64), 192, perm1, sp1, yg1)
             (ang1, ang0)[q][...] = dot(h2, z[(i + 1) % NB])
 
     loop(NB, mix_permute)
     ang0[...] = dot(h2, z[0])
     loop(NB // 2, features_permute)
 
-    each(NB, lambda k: st_copy(k).wait())
-    stat2[0] = jnp.sum(stat[...], axis=0)
-
-    def st2_copy(k):
-        return remote(st_dev(k), stat2.at[0], stat2.at[k], st2_send.at[k], st2_recv.at[k])
-
-    each(NS, lambda k: st2_copy(k).start())
-
-    loop(NB, lambda i: mix_across(i, y1, bc1, z))
-
-    each(NS, lambda k: st2_copy(k).wait())
-    totals = jnp.sum(stat2[...], axis=0)
-    norm_old, d_norm = totals[:, :T], totals[:, T:]
+    loop(NB, lambda i: mix_across(i, yg1, bc1, z))
+
     both(lambda a, k: d2_copy(a, k).wait_recv())
 
     def project(a):
@@ -335,7 +312,7 @@
             hi, lo = split(block)
             big = dot(jnp.concatenate([hi, lo], axis=0), fh[s, a])
             part += big[:T] + (big[T:] + dot(hi, fl[s, a]))
-        pacc[...] += part
+        pacc[:T] += part
 
     def features_project(j):
         for q in range(2):
@@ -344,7 +321,6 @@
             (ang1, ang0)[q][...] = dot(h2, z[(i + 1) % NB])
             project(i)
 
-    pacc[...] = jnp.zeros_like(pacc)
     ang0[...] = dot(h2, z[0])
     loop(NB // 2, features_project)
 
@@ -361,12 +337,14 @@
     each(4, lambda k: p2_copy(k).start())
     px[0] = pchip[...]
     each(4, lambda k: p2_copy(k).wait_recv())
-    projected = (px[0] + px[1]) + (px[2] + px[3])
+    summed = (px[0] + px[1]) + (px[2] + px[3])
+    projected = summed[:T]
     p_hi, p_lo = split(projected)
     p_both = jnp.concatenate([p_hi, p_lo], axis=0)
 
     pp_row = row_sums(jnp.square(projected))
-    pp[0] = jnp.concatenate([pp_row, pp_row], axis=1)
+    pp[0, :8] = jnp.concatenate([pp_row, pp_row], axis=1)
+    pp[0, 8:] = summed[T:, :128]
 
     def pp_copy(k):
         return remote(ex_dev(0, k), pp.at[0], pp.at[k], pp_send.at[k], pp_recv.at[k])
@@ -423,9 +401,11 @@
     each(4, forward_out)
 
     each(4, lambda k: pp2_copy(k).wait())
-    p_norm = jnp.sum(pp2[...], axis=0)[:, :T]
+    totals = jnp.sum(pp2[...], axis=0)
+    p_norm, norm_old, d_norm = totals[:8, :T], totals[8:, :T], totals[8:, T:]
     step = column(norm_old / (RIDGE * d_norm + p_norm))
-    wide[0] = jnp.broadcast_to(step, (T, 128))
+    for s in range(2):
+        wide[0, :, s, :] = jnp.broadcast_to(step, (T, BLK))
     step_copy = pltpu.make_async_copy(wide.at[0], step_out, out_sem.at[0])
     step_copy.start()
 
@@ -468,7 +448,9 @@
     app_copy.wait()
     each(NS, lambda k: n2_copy(k).wait())
     norm_new = jnp.sum(nn2[...], axis=0)[:, :T]
-    wide[1] = jnp.broadcast_to(column(norm_new / (norm_old + EPSILON)), (T, 128))
+    conjugacy = column(norm_new / (norm_old + EPSILON))
+    for s in range(2):
+        wide[1, :, s, :] = jnp.broadcast_to(conjugacy, (T, BLK))
     conj_copy = pltpu.make_async_copy(wide.at[1], conj_out, out_sem.at[2])
     conj_copy.start()
     conj_copy.wait()
@@ -481,11 +463,7 @@
     block, tile = (T, BLK), (8, 128)
     applied, step, conjugacy = pl.pallas_call(
         kernel,
-        out_shape=[
-            jax.ShapeDtypeStruct(direction.shape, f32),
-            jax.ShapeDtypeStruct((T, 128), f32),
-            jax.ShapeDtypeStruct((T, 128), f32),
-        ],
+        out_shape=[jax.ShapeDtypeStruct(direction.shape, f32)] * 3,
         in_specs=[hbm] * 8,
         out_specs=[hbm] * 3,
         scratch_shapes=[
@@ -496,14 +474,18 @@
             vmem((2, D), f32),
             vmem(direction.shape, f32),
             vmem(direction.shape, f32),
+            vmem((2, D), jnp.int32),
+            vmem((2, D), jnp.int32),
             pltpu.SMEM((D,), jnp.int32),
             pltpu.SMEM((D,), jnp.int32),
-            dma((9,)),
+            dma((8,)),
+            dma((2,)),
             dma((3,)),
             vmem((D, BLK), f32),
-            vmem((2, D, 128), f32),
-            vmem((D, BLK), f32),
-            vmem((2, D, 128), f32),
+            vmem((2 * D, 128), f32),
+            vmem((2 * D, 128), f32),
+            vmem((2 * D, 128), f32),
+            vmem((2 * D, 128), f32),
             vmem((NB, 2 * BLK, BLK), bf16),
             vmem((2, NB, BLK, BLK), bf16),
             vmem((2, NB, BLK, BLK), bf16),
@@ -514,12 +496,10 @@
             vmem((BLK, BLK), f32),
             vmem((NB,) + block, f32),
             vmem((NB,) + block, f32),
-            vmem((NB,) + tile, f32),
-            vmem((NS,) + tile, f32),
-            vmem(block, f32),
-            vmem(block, f32),
-            vmem(block, f32),
-            vmem((4,) + block, f32),
+            vmem((T + 8, BLK), f32),
+            vmem((T + 8, BLK), f32),
+            vmem((T + 8, BLK), f32),
+            vmem((4, T + 8, BLK), f32),
             vmem((4, 4) + block, f32),
             vmem((4, 4) + block, f32),
             vmem((4, 4) + block, f32),
@@ -529,13 +509,12 @@
             vmem((4,) + block, f32),
             vmem((4,) + block, f32),
             vmem(direction.shape, f32),
-            vmem((2, T, 128), f32),
-            vmem((4,) + tile, f32),
-            vmem((4,) + tile, f32),
+            vmem((2,) + direction.shape, f32),
+            vmem((4, 16, 128), f32),
+            vmem((4, 16, 128), f32),
             vmem((NB,) + tile, f32),
             vmem((NS,) + tile, f32),
             dma((2, 4)), dma((2, 4)), dma((2, 4)), dma((2, 4)),
-            dma((NB,)), dma((NB,)), dma((NS,)), dma((NS,)),
             dma, dma, dma((4,)), dma((4,)),
             dma((2, 4, 4)), dma((2, 4, 4)), dma((2, 4)), dma((2, 4)),
             dma((4,)), dma((4,)), dma((4,)), dma((4,)),
@@ -545,8 +524,6 @@
             collective_id=0, has_side_effects=True, vmem_limit_bytes=60 * 2**20
         ),
     )(embeddings, sign_bits, permutation, gaussian, scaling, phases, residual, direction)
-    step = step[:, :1, None]
-    conjugacy = conjugacy[:, :1, None]
     residual_next = residual - step * applied
     return solution + step * direction, residual_next, residual_next + conjugacy * direction
 

time: 77.9 us -> 74.1 us (0.951)
  Pallas kernels: 74.2 us -> 71.4 us
  local copies, waits for them, and re-layouts: 0.89 us -> 0.01 us
    pallas_call x1, Pallas kernels: 74.2 us -> 71.4 us  [local(): pl.pallas_call(kernel, out_shape=[jax.ShapeDtypeStruct(direction.shape, f...]
    slice x1 -> x0, local copies, waits for them, and re-layouts: 0.88 us -> none  [local(): conjugacy = conjugacy[:, :1, None]]
where the time goes in v4:
time: 74.1 us; the launch traced here: 73.9 us
  Pallas kernels  71.4 us (96%)
  other arithmetic  1.82 us (2%)
    pallas_call x1, Pallas kernels, local(): pl.pallas_call(kernel, out_shape=[jax.ShapeDtypeStruct(direction.shape, f...  71.4 us
    add x1, other arithmetic, local(): residual_next + conjugacy * direction  1.82 us

profile of v4, /device:TPU:1, one launch (start us, length us, event | category | flops | bytes accessed | tf_op | source)
XLA Modules:
  0.0 73.9 jit_solution(4297945005887231620)
XLA Ops:
  0.6 0.0 copy-start.1
  0.6 0.0 copy-start
  0.7 0.0 copy-start.2
  0.7 71.4 %shard_map.112 = (f32[64,2,256]{2,1,0:T(2,128)}, f32[64,2,256]{2,1,0:T(2,128)}, f32[64,2,256]{2,1,0:T(2,128)}) custom-call(bf16[4096,256]{1,0:T(8,128)(2,1)} %emb_h.1, s32[2,4096]{1,0:T(2,128)} %sign_h.1, s32[2,4096]{1,0:T(2,128)} %perm_h.1, f32[2,4096]{1,0:T(2,128)} %gauss_h.1, f32[2,4096]{1,0:T(2,128)} %scale_h.1, f32[2,4096]{1,0:T(2,128)} %phase_h.1, ...), custom_call_target="tpu_custom_call" | custom-call | tf_op jit(solution)/shard_map/pallas_call | solution.py:464
  72.0 0.0 copy-done.1
  72.1 0.0 copy-done
  72.1 0.0 copy-done.2
  72.1 1.8 %multiply_add_fusion = (f32[16,8,256]{2,1,0:T(8,128)}, f32[16,8,256]{2,1,0:T(8,128)}, f32[16,8,256]{2,1,0:T(8,128)}) fusion(f32[16,8,256]{2,1,0:T(8,128)} %bitcast.17, f32[16,8,256]{2,1,0:T(8,128)S(1)} %bitcast.10, f32[16,8,256]{2,1,0:T(8,128)S(1)} %bitcast.9, f32[16,8,256]{2,1,0:T(8,128)} %bitcast.16, f32[16,8,256]{2,1,0:T(8,128)} %bitcast.15, ...), kind=kLoop, calls=%fused_computation | loop fusion | flops 196608 | bytes 1179648 | tf_op jit(solution)/shard_map/add | solution.py:528
Async XLA Ops:
  0.6 71.4 %copy-start.1 = (f32[64,2,256]{2,1,0:T(2,128)S(1)}, f32[64,2,256]{2,1,0:T(2,128)}, u32[]{:S(2)}) copy-start(f32[64,2,256]{2,1,0:T(2,128)} %dire_h.1) | copy-start | bytes 393220
  0.6 71.4 %copy-start = (f32[64,2,256]{2,1,0:T(2,128)S(1)}, f32[64,2,256]{2,1,0:T(2,128)}, u32[]{:S(2)}) copy-start(f32[64,2,256]{2,1,0:T(2,128)} %res_h.1) | copy-start | bytes 393220
  0.7 71.4 %copy-start.2 = (f32[64,2,256]{2,1,0:T(2,128)S(1)}, f32[64,2,256]{2,1,0:T(2,128)}, u32[]{:S(2)}) copy-start(f32[64,2,256]{2,1,0:T(2,128)} %param.15) | copy-start | bytes 393220

commit v5 on v4

--- a/solution.py
+++ b/solution.py
@@ -59,10 +59,9 @@
 
 
 def row_sums(x):
-    ones = jnp.ones((8, x.shape[1]), f32)
-    return lax.dot_general(
-        ones, x, (((1,), (1,)), ((), ())), precision=lax.Precision.HIGHEST, preferred_element_type=f32
-    )
+    hi, lo = split(x)
+    ones = jnp.ones((8, x.shape[1]), bf16)
+    return dot_t(ones, hi) + dot_t(ones, lo)
 
 
 def column(row):
@@ -235,27 +234,6 @@
     inputs[3].wait()
     loop(NB, lambda a: spread_block(0, a, sign, emb, h, y), 4)
     loop(32, lambda r: spread_across(r, y, sp), 2)
-    pl.semaphore_wait(barrier, NB - 1 + NS - 1)
-
-    def d1_copy(a, k):
-        if a:
-            return remote(ex_dev(0, k), da.at[own_a], da.at[own_a], d1_send.at[0, k], d1_recv.at[0, k])
-        return remote(ex_dev(k, 0), db.at[own_b], db.at[own_b], d1_send.at[1, k], d1_recv.at[1, k])
-
-    def d2_copy(a, k):
-        four_a, four_b = da.at[pl.ds(ez * 4, 4)], db.at[pl.ds(ey * 4, 4)]
-        if a:
-            return remote(ex_dev(k, 0), four_a, four_a, d2_send.at[0, k], d2_recv.at[0, k])
-        return remote(ex_dev(0, k), four_b, four_b, d2_send.at[1, k], d2_recv.at[1, k])
-
-    def both(f):
-        def go(k):
-            f(True, k)
-            f(False, k)
-
-        each(4, go)
-
-    both(lambda a, k: d1_copy(a, k).start())
 
     r2 = row_sums(jnp.concatenate([jnp.square(res[:, s, :]) for s in range(2)], axis=1))
     d2 = row_sums(jnp.concatenate([jnp.square(dire[:, s, :]) for s in range(2)], axis=1))
@@ -281,11 +259,32 @@
         for q in range(2):
             spread_parameters(1, 2 * i + q, col, bc1)
 
-    loop(8, permute_spread)
-    loop(8, permute_spread_across)
-
+    loop(3, permute_spread)
+    pl.semaphore_wait(barrier, NB - 1 + NS - 1)
+    def d1_copy(a, k):
+        if a:
+            return remote(ex_dev(0, k), da.at[own_a], da.at[own_a], d1_send.at[0, k], d1_recv.at[0, k])
+        return remote(ex_dev(k, 0), db.at[own_b], db.at[own_b], d1_send.at[1, k], d1_recv.at[1, k])
+
+    def d2_copy(a, k):
+        four_a, four_b = da.at[pl.ds(ez * 4, 4)], db.at[pl.ds(ey * 4, 4)]
+        if a:
+            return remote(ex_dev(k, 0), four_a, four_a, d2_send.at[0, k], d2_recv.at[0, k])
+        return remote(ex_dev(0, k), four_b, four_b, d2_send.at[1, k], d2_recv.at[1, k])
+
+    def both(f):
+        def go(k):
+            f(True, k)
+            f(False, k)
+
+        each(4, go)
+
+    both(lambda a, k: d1_copy(a, k).start())
+
+    loop(8 - 3, lambda i: permute_spread(3 + i))
     both(lambda a, k: d1_copy(a, k).wait_recv())
     both(lambda a, k: d2_copy(a, k).start())
+    loop(8, permute_spread_across)
 
     def mix_permute(i):
         mix_across(i, yg, bc0, z)
@@ -303,8 +302,6 @@
     loop(NB // 2, features_permute)
 
     loop(NB, lambda i: mix_across(i, yg1, bc1, z))
-
-    both(lambda a, k: d2_copy(a, k).wait_recv())
 
     def project(a):
         part = 0.0
@@ -322,6 +319,7 @@
             project(i)
 
     ang0[...] = dot(h2, z[0])
+    both(lambda a, k: d2_copy(a, k).wait_recv())
     loop(NB // 2, features_project)
 
     def p1_copy():
@@ -424,14 +422,16 @@
     def n1_copy(k):
         return remote(ex_k(k), nn.at[0], nn.at[k], n1_send.at[k], n1_recv.at[k])
 
-    each(NB, lambda k: n1_copy(k).start())
+    for k in (10, 9, 11, 6, 14, 8, 2, 5, 7, 13, 15, 1, 3, 4, 12):
+        n1_copy(k).start()
     each(NB, lambda k: n1_copy(k).wait())
     nn2[0] = jnp.sum(nn[...], axis=0)
 
     def n2_copy(k):
         return remote(st_dev(k), nn2.at[0], nn2.at[k], n2_send.at[k], n2_recv.at[k])
 
-    each(NS, lambda k: n2_copy(k).start())
+    for k in (4, 5, 3, 2, 6, 7, 1):
+        n2_copy(k).start()
     both(lambda a, k: d1_copy(a, k).wait_send())
     both(lambda a, k: d2_copy(a, k).wait_send())
     p1_copy().wait_send()

time: 74.1 us -> 73.1 us (0.987)
  Pallas kernels: 71.4 us -> 70.4 us
    pallas_call x1, Pallas kernels: 71.4 us -> 70.4 us  [local(): pl.pallas_call(kernel, out_shape=[jax.ShapeDtypeStruct(direction.shape, f...]
where the time goes in v5:
time: 73.1 us; the launch traced here: 72.9 us
  Pallas kernels  70.4 us (96%)
  other arithmetic  1.82 us (2%)
    pallas_call x1, Pallas kernels, local(): pl.pallas_call(kernel, out_shape=[jax.ShapeDtypeStruct(direction.shape, f...  70.4 us
    add x1, other arithmetic, local(): residual_next + conjugacy * direction  1.82 us

profile of v5, /device:TPU:1, one launch (start us, length us, event | category | flops | bytes accessed | tf_op | source)
XLA Modules:
  0.0 72.9 jit_solution(9704966488157411046)
XLA Ops:
  0.6 0.0 copy-start.1
  0.6 0.0 copy-start
  0.7 0.0 copy-start.2
  0.7 70.4 %shard_map.112 = (f32[64,2,256]{2,1,0:T(2,128)}, f32[64,2,256]{2,1,0:T(2,128)}, f32[64,2,256]{2,1,0:T(2,128)}) custom-call(bf16[4096,256]{1,0:T(8,128)(2,1)} %emb_h.1, s32[2,4096]{1,0:T(2,128)} %sign_h.1, s32[2,4096]{1,0:T(2,128)} %perm_h.1, f32[2,4096]{1,0:T(2,128)} %gauss_h.1, f32[2,4096]{1,0:T(2,128)} %scale_h.1, f32[2,4096]{1,0:T(2,128)} %phase_h.1, ...), custom_call_target="tpu_custom_call" | custom-call | tf_op jit(solution)/shard_map/pallas_call | solution.py:464
  71.1 0.0 copy-done.1
  71.1 0.0 copy-done
  71.1 0.0 copy-done.2
  71.1 1.8 %multiply_add_fusion = (f32[16,8,256]{2,1,0:T(8,128)}, f32[16,8,256]{2,1,0:T(8,128)}, f32[16,8,256]{2,1,0:T(8,128)}) fusion(f32[16,8,256]{2,1,0:T(8,128)} %bitcast.17, f32[16,8,256]{2,1,0:T(8,128)S(1)} %bitcast.10, f32[16,8,256]{2,1,0:T(8,128)S(1)} %bitcast.9, f32[16,8,256]{2,1,0:T(8,128)} %bitcast.16, f32[16,8,256]{2,1,0:T(8,128)} %bitcast.15, ...), kind=kLoop, calls=%fused_computation | loop fusion | flops 196608 | bytes 1179648 | tf_op jit(solution)/shard_map/add | solution.py:528
Async XLA Ops:
  0.6 70.4 %copy-start.1 = (f32[64,2,256]{2,1,0:T(2,128)S(1)}, f32[64,2,256]{2,1,0:T(2,128)}, u32[]{:S(2)}) copy-start(f32[64,2,256]{2,1,0:T(2,128)} %dire_h.1) | copy-start | bytes 393220
  0.6 70.4 %copy-start = (f32[64,2,256]{2,1,0:T(2,128)S(1)}, f32[64,2,256]{2,1,0:T(2,128)}, u32[]{:S(2)}) copy-start(f32[64,2,256]{2,1,0:T(2,128)} %res_h.1) | copy-start | bytes 393220
  0.7 70.4 %copy-start.2 = (f32[64,2,256]{2,1,0:T(2,128)S(1)}, f32[64,2,256]{2,1,0:T(2,128)}, u32[]{:S(2)}) copy-start(f32[64,2,256]{2,1,0:T(2,128)} %param.15) | copy-start | bytes 393220

commit v6 on v5

--- a/solution.py
+++ b/solution.py
@@ -163,9 +163,9 @@
     applied_out, step_out, conj_out,
     emb, sign, gauss, scale, phase, res, dire, pv, pv2, perm0, perm1, in_sem, perm_sem, out_sem,
     y, sp, yg, sp1, yg1, z, fh, fl, col, bc0, bc1, ang0, ang1,
-    da, db, pacc, psib, pchip, px, sa, sb, ra1, rb1, sa2, sb2, ra2, rb2, app, wide, pp, pp2, nn, nn2,
+    da, db, pacc, psib, pchip, px, sa, sb, ra1, rb1, relay, sa2, sb2, ra2, rb2, app, wide, pp, pp2, nn, nn2,
     d1_send, d1_recv, d2_send, d2_recv,
-    p1_send, p1_recv, p2_send, p2_recv, i1_send, i1_recv, i2_send, i2_recv,
+    p1_send, p1_recv, p2_send, p2_recv, i1_send, i1_recv, i2_send, i2_recv, r_send, r_recv,
     pp_send, pp_recv, pp2_send, pp2_recv, n1_send, n1_recv, n2_send, n2_recv,
 ):
     ex = lax.axis_index("ex")
@@ -365,17 +365,46 @@
             ex_dev(near, 0), sb.at[near, far], rb1.at[near, far], i1_send.at[1, near, far], i1_recv.at[1, near, far]
         )
 
-    def image_out(i):
-        far, near = (i // 4 + 1) % 4, (i + 1) % 4
+    def via(far):
+        return 1 + 2 * (far % 2)
+
+    def relay_copy(a, far):
+        if a:
+            return remote(ex_dev(0, via(far)), sa.at[2, far], relay.at[0, far], r_send.at[0, far], r_recv.at[0, far])
+        return remote(ex_dev(via(far), 0), sb.at[2, far], relay.at[1, far], r_send.at[1, far], r_recv.at[1, far])
+
+    def images(near, far):
         sa[near, far] = image(0, ring(ez, far) * 4 + ring(ey, near))
         sb[near, far] = image(1, ring(ez, near) * 4 + ring(ey, far))
 
-        @pl.when(near > 0)
-        def _():
-            i1_copy(True, near, far).start()
-            i1_copy(False, near, far).start()
-
-    each(16, image_out, 0)
+    def start_images(near, far):
+        i1_copy(True, near, far).start()
+        i1_copy(False, near, far).start()
+
+    def opposite(i):
+        far = (i + 1) % 4
+        images(2, far)
+        relay_copy(True, far).start()
+        relay_copy(False, far).start()
+
+    def direct(i):
+        far = (i + 1) % 4
+        images(4 - via(far), far)
+        start_images(4 - via(far), far)
+
+    def relayed(i):
+        far = (i + 1) % 4
+        relay_copy(True, far).wait_recv()
+        relay_copy(False, far).wait_recv()
+        sa[via(far), far] += relay[0, far]
+        sb[via(far), far] += relay[1, far]
+        start_images(via(far), far)
+
+    each(4, opposite, 0)
+    each(4, direct, 0)
+    each(4, lambda i: images(via((i + 1) % 4), (i + 1) % 4), 0)
+    each(4, relayed, 0)
+    each(4, lambda far: images(0, far), 0)
 
     each(4, lambda k: pp_copy(k).wait())
     pp2[0] = jnp.sum(pp[...], axis=0)
@@ -388,8 +417,9 @@
 
     def forward(far):
         for a, src, got, out in ((True, sa, ra1, sa2), (False, sb, rb1, sb2)):
-            each(4, lambda near: i1_copy(a, near, far).wait_recv())
-            out[far] = (src[0, far] + got[1, far]) + (got[2, far] + got[3, far])
+            i1_copy(a, 1, far).wait_recv()
+            i1_copy(a, 3, far).wait_recv()
+            out[far] = src[0, far] + (got[1, far] + got[3, far])
 
     def forward_out(far):
         forward(far)
@@ -437,12 +467,13 @@
     p1_copy().wait_send()
     each(4, lambda k: p2_copy(k).wait_send())
 
-    def i1_sent(i):
-        near, far = i // 4 + 1, i % 4
-        i1_copy(True, near, far).wait_send()
-        i1_copy(False, near, far).wait_send()
-
-    each(12, i1_sent, 0)
+    def i1_sent(far):
+        for a in (True, False):
+            relay_copy(a, far).wait_send()
+            i1_copy(a, 1, far).wait_send()
+            i1_copy(a, 3, far).wait_send()
+
+    each(4, i1_sent, 0)
     both(lambda a, k: i2_copy(a, k).wait_send())
     step_copy.wait()
     app_copy.wait()
@@ -504,6 +535,7 @@
             vmem((4, 4) + block, f32),
             vmem((4, 4) + block, f32),
             vmem((4, 4) + block, f32),
+            vmem((2, 4) + block, f32),
             vmem((4,) + block, f32),
             vmem((4,) + block, f32),
             vmem((4,) + block, f32),
@@ -516,7 +548,7 @@
             vmem((NS,) + tile, f32),
             dma((2, 4)), dma((2, 4)), dma((2, 4)), dma((2, 4)),
             dma, dma, dma((4,)), dma((4,)),
-            dma((2, 4, 4)), dma((2, 4, 4)), dma((2, 4)), dma((2, 4)),
+            dma((2, 4, 4)), dma((2, 4, 4)), dma((2, 4)), dma((2, 4)), dma((2, 4)), dma((2, 4)),
             dma((4,)), dma((4,)), dma((4,)), dma((4,)),
             dma((NB,)), dma((NB,)), dma((NS,)), dma((NS,)),
         ],

time: 73.1 us -> 71.4 us (0.977)
  Pallas kernels: 70.4 us -> 68.7 us
    pallas_call x1, Pallas kernels: 70.4 us -> 68.7 us  [local(): pl.pallas_call(kernel, out_shape=[jax.ShapeDtypeStruct(direction.shape, f...]
where the time goes in v6:
time: 71.4 us; the launch traced here: 71.2 us
  Pallas kernels  68.7 us (96%)
  other arithmetic  1.82 us (3%)
    pallas_call x1, Pallas kernels, local(): pl.pallas_call(kernel, out_shape=[jax.ShapeDtypeStruct(direction.shape, f...  68.7 us
    add x1, other arithmetic, local(): residual_next + conjugacy * direction  1.82 us

profile of v6, /device:TPU:1, one launch (start us, length us, event | category | flops | bytes accessed | tf_op | source)
XLA Modules:
  0.0 71.2 jit_solution(13463095275353492597)
XLA Ops:
  0.6 0.0 copy-start.1
  0.6 0.0 copy-start
  0.7 0.0 copy-start.2
  0.7 68.7 %shard_map.112 = (f32[64,2,256]{2,1,0:T(2,128)}, f32[64,2,256]{2,1,0:T(2,128)}, f32[64,2,256]{2,1,0:T(2,128)}) custom-call(bf16[4096,256]{1,0:T(8,128)(2,1)} %emb_h.1, s32[2,4096]{1,0:T(2,128)} %sign_h.1, s32[2,4096]{1,0:T(2,128)} %perm_h.1, f32[2,4096]{1,0:T(2,128)} %gauss_h.1, f32[2,4096]{1,0:T(2,128)} %scale_h.1, f32[2,4096]{1,0:T(2,128)} %phase_h.1, ...), custom_call_target="tpu_custom_call" | custom-call | tf_op jit(solution)/shard_map/pallas_call | solution.py:495
  69.3 0.0 copy-done.1
  69.4 0.0 copy-done
  69.4 0.0 copy-done.2
  69.4 1.8 %multiply_add_fusion = (f32[16,8,256]{2,1,0:T(8,128)}, f32[16,8,256]{2,1,0:T(8,128)}, f32[16,8,256]{2,1,0:T(8,128)}) fusion(f32[16,8,256]{2,1,0:T(8,128)} %bitcast.17, f32[16,8,256]{2,1,0:T(8,128)S(1)} %bitcast.10, f32[16,8,256]{2,1,0:T(8,128)S(1)} %bitcast.9, f32[16,8,256]{2,1,0:T(8,128)} %bitcast.16, f32[16,8,256]{2,1,0:T(8,128)} %bitcast.15, ...), kind=kLoop, calls=%fused_computation | loop fusion | flops 196608 | bytes 1179648 | tf_op jit(solution)/shard_map/add | solution.py:560
Async XLA Ops:
  0.6 68.7 %copy-start.1 = (f32[64,2,256]{2,1,0:T(2,128)S(1)}, f32[64,2,256]{2,1,0:T(2,128)}, u32[]{:S(2)}) copy-start(f32[64,2,256]{2,1,0:T(2,128)} %dire_h.1) | copy-start | bytes 393220
  0.6 68.7 %copy-start = (f32[64,2,256]{2,1,0:T(2,128)S(1)}, f32[64,2,256]{2,1,0:T(2,128)}, u32[]{:S(2)}) copy-start(f32[64,2,256]{2,1,0:T(2,128)} %res_h.1) | copy-start | bytes 393220
  0.7 68.7 %copy-start.2 = (f32[64,2,256]{2,1,0:T(2,128)S(1)}, f32[64,2,256]{2,1,0:T(2,128)}, u32[]{:S(2)}) copy-start(f32[64,2,256]{2,1,0:T(2,128)} %param.15) | copy-start | bytes 393220

commit v7 on v6

--- a/solution.py
+++ b/solution.py
@@ -188,12 +188,12 @@
             src_ref=src, dst_ref=dst, send_sem=send, recv_sem=recv, device_id=dev, device_id_type=MESH
         )
 
-    def each(n, f, first=1):
+    def each(n, f, first=1, unroll=1):
         def body(k, _):
             f(k)
             return 0
 
-        lax.fori_loop(first, n, body, 0)
+        lax.fori_loop(first, n, body, 0, unroll=unroll)
 
     def ex_k(k):
         return ex_dev(k // 4, k % 4)
@@ -202,7 +202,7 @@
         pltpu.make_async_copy(src, dst, in_sem.at[i])
         for i, (src, dst) in enumerate(
             [
-                (dire_h, dire), (res_h, res), (sign_h, sign), (emb_h, emb), (gauss_h, gauss),
+                (emb_h, emb), (sign_h, sign), (dire_h, dire), (res_h, res), (gauss_h, gauss),
                 (scale_h, scale), (phase_h, phase), (perm_h, pv),
             ]
         )
@@ -217,12 +217,6 @@
     hb = h.astype(bf16)
     h2 = jnp.concatenate([hb, hb], axis=1)
 
-    inputs[0].wait()
-    inputs[1].wait()
-    own_a, own_b = ex, ey * 4 + ez
-    da[own_a] = dire[:, 0, :]
-    db[own_b] = dire[:, 1, :]
-
     inputs[7].wait()
     pv2[...] = 2 * pv[...]
     perm_copies = [
@@ -230,10 +224,16 @@
     ]
     for c in perm_copies:
         c.start()
+    inputs[0].wait()
+    inputs[1].wait()
+    loop(NB, lambda a: spread_block(0, a, sign, emb, h, y), 4)
+    loop(32, lambda r: spread_across(r, y, sp), 2)
+
     inputs[2].wait()
     inputs[3].wait()
-    loop(NB, lambda a: spread_block(0, a, sign, emb, h, y), 4)
-    loop(32, lambda r: spread_across(r, y, sp), 2)
+    own_a, own_b = ex, ey * 4 + ez
+    da[own_a] = dire[:, 0, :]
+    db[own_b] = dire[:, 1, :]
 
     r2 = row_sums(jnp.concatenate([jnp.square(res[:, s, :]) for s in range(2)], axis=1))
     d2 = row_sums(jnp.concatenate([jnp.square(dire[:, s, :]) for s in range(2)], axis=1))
@@ -259,7 +259,7 @@
         for q in range(2):
             spread_parameters(1, 2 * i + q, col, bc1)
 
-    loop(3, permute_spread)
+    loop(1, permute_spread)
     pl.semaphore_wait(barrier, NB - 1 + NS - 1)
     def d1_copy(a, k):
         if a:
@@ -281,7 +281,7 @@
 
     both(lambda a, k: d1_copy(a, k).start())
 
-    loop(8 - 3, lambda i: permute_spread(3 + i))
+    loop(8 - 1, lambda i: permute_spread(1 + i))
     both(lambda a, k: d1_copy(a, k).wait_recv())
     both(lambda a, k: d2_copy(a, k).start())
     loop(8, permute_spread_across)
@@ -301,7 +301,7 @@
     ang0[...] = dot(h2, z[0])
     loop(NB // 2, features_permute)
 
-    loop(NB, lambda i: mix_across(i, yg1, bc1, z))
+    loop(NB, lambda i: mix_across(i, yg1, bc1, z), 2)
 
     def project(a):
         part = 0.0
@@ -340,17 +340,11 @@
     p_hi, p_lo = split(projected)
     p_both = jnp.concatenate([p_hi, p_lo], axis=0)
 
-    pp_row = row_sums(jnp.square(projected))
-    pp[0, :8] = jnp.concatenate([pp_row, pp_row], axis=1)
-    pp[0, 8:] = summed[T:, :128]
-
     def pp_copy(k):
         return remote(ex_dev(0, k), pp.at[0], pp.at[k], pp_send.at[k], pp_recv.at[k])
 
     def pp2_copy(k):
         return remote(ex_dev(k, 0), pp2.at[0], pp2.at[k], pp2_send.at[k], pp2_recv.at[k])
-
-    each(4, lambda k: pp_copy(k).start())
 
     def image(s, e):
         big = dot_t(p_both, fh[s, e])
@@ -400,11 +394,17 @@
         sb[via(far), far] += relay[1, far]
         start_images(via(far), far)
 
-    each(4, opposite, 0)
-    each(4, direct, 0)
-    each(4, lambda i: images(via((i + 1) % 4), (i + 1) % 4), 0)
+    each(4, opposite, 0, 4)
+
+    pp_row = row_sums(jnp.square(projected))
+    pp[0, :8] = jnp.concatenate([pp_row, pp_row], axis=1)
+    pp[0, 8:] = summed[T:, :128]
+
+    each(4, lambda k: pp_copy(k).start())
+    each(4, direct, 0, 4)
+    each(4, lambda i: images(via((i + 1) % 4), (i + 1) % 4), 0, 4)
     each(4, relayed, 0)
-    each(4, lambda far: images(0, far), 0)
+    each(4, lambda far: images(0, far), 0, 4)
 
     each(4, lambda k: pp_copy(k).wait())
     pp2[0] = jnp.sum(pp[...], axis=0)

time: 71.4 us -> 69.9 us (0.979)
  Pallas kernels: 68.7 us -> 67.2 us
    pallas_call x1, Pallas kernels: 68.7 us -> 67.2 us  [local(): pl.pallas_call(kernel, out_shape=[jax.ShapeDtypeStruct(direction.shape, f...]
where the time goes in v7:
time: 69.9 us; the launch traced here: 69.8 us
  Pallas kernels  67.2 us (96%)
  other arithmetic  1.82 us (3%)
    pallas_call x1, Pallas kernels, local(): pl.pallas_call(kernel, out_shape=[jax.ShapeDtypeStruct(direction.shape, f...  67.2 us
    add x1, other arithmetic, local(): residual_next + conjugacy * direction  1.82 us

profile of v7, /device:TPU:1, one launch (start us, length us, event | category | flops | bytes accessed | tf_op | source)
XLA Modules:
  0.0 69.8 jit_solution(990598650982400630)
XLA Ops:
  0.6 0.0 copy-start.1
  0.6 0.0 copy-start
  0.7 0.0 copy-start.2
  0.7 67.2 %shard_map.112 = (f32[64,2,256]{2,1,0:T(2,128)}, f32[64,2,256]{2,1,0:T(2,128)}, f32[64,2,256]{2,1,0:T(2,128)}) custom-call(bf16[4096,256]{1,0:T(8,128)(2,1)} %emb_h.1, s32[2,4096]{1,0:T(2,128)} %sign_h.1, s32[2,4096]{1,0:T(2,128)} %perm_h.1, f32[2,4096]{1,0:T(2,128)} %gauss_h.1, f32[2,4096]{1,0:T(2,128)} %scale_h.1, f32[2,4096]{1,0:T(2,128)} %phase_h.1, ...), custom_call_target="tpu_custom_call" | custom-call | tf_op jit(solution)/shard_map/pallas_call | solution.py:495
  67.9 0.0 copy-done.1
  67.9 0.0 copy-done
  67.9 0.0 copy-done.2
  67.9 1.8 %multiply_add_fusion = (f32[16,8,256]{2,1,0:T(8,128)}, f32[16,8,256]{2,1,0:T(8,128)}, f32[16,8,256]{2,1,0:T(8,128)}) fusion(f32[16,8,256]{2,1,0:T(8,128)} %bitcast.17, f32[16,8,256]{2,1,0:T(8,128)S(1)} %bitcast.10, f32[16,8,256]{2,1,0:T(8,128)S(1)} %bitcast.9, f32[16,8,256]{2,1,0:T(8,128)} %bitcast.16, f32[16,8,256]{2,1,0:T(8,128)} %bitcast.15, ...), kind=kLoop, calls=%fused_computation | loop fusion | flops 196608 | bytes 1179648 | tf_op jit(solution)/shard_map/add | solution.py:560
Async XLA Ops:
  0.6 67.3 %copy-start.1 = (f32[64,2,256]{2,1,0:T(2,128)S(1)}, f32[64,2,256]{2,1,0:T(2,128)}, u32[]{:S(2)}) copy-start(f32[64,2,256]{2,1,0:T(2,128)} %dire_h.1) | copy-start | bytes 393220
  0.6 67.3 %copy-start = (f32[64,2,256]{2,1,0:T(2,128)S(1)}, f32[64,2,256]{2,1,0:T(2,128)}, u32[]{:S(2)}) copy-start(f32[64,2,256]{2,1,0:T(2,128)} %res_h.1) | copy-start | bytes 393220
  0.7 67.3 %copy-start.2 = (f32[64,2,256]{2,1,0:T(2,128)S(1)}, f32[64,2,256]{2,1,0:T(2,128)}, u32[]{:S(2)}) copy-start(f32[64,2,256]{2,1,0:T(2,128)} %param.15) | copy-start | bytes 393220

commit v8 on v7

--- a/solution.py
+++ b/solution.py
@@ -297,7 +297,7 @@
             permute(pl.multiple_of(16 * 64 + i * 192, 64), 192, perm1, sp1, yg1)
             (ang1, ang0)[q][...] = dot(h2, z[(i + 1) % NB])
 
-    loop(NB, mix_permute)
+    loop(NB, mix_permute, 2)
     ang0[...] = dot(h2, z[0])
     loop(NB // 2, features_permute)
 
@@ -332,7 +332,8 @@
     def p2_copy(k):
         return remote(st_dev(2 * k), pchip, px.at[k], p2_send.at[k], p2_recv.at[k])
 
-    each(4, lambda k: p2_copy(k).start())
+    for k in (2, 1, 3):
+        p2_copy(k).start()
     px[0] = pchip[...]
     each(4, lambda k: p2_copy(k).wait_recv())
     summed = (px[0] + px[1]) + (px[2] + px[3])

time: 69.9 us -> 69.9 us (level)
  no operation moved by 1% of the time
where the time goes in v8:
time: 69.9 us; the launch traced here: 69.8 us
  Pallas kernels  67.2 us (96%)
  other arithmetic  1.82 us (3%)
    pallas_call x1, Pallas kernels, local(): pl.pallas_call(kernel, out_shape=[jax.ShapeDtypeStruct(direction.shape, f...  67.2 us
    add x1, other arithmetic, local(): residual_next + conjugacy * direction  1.82 us

profile of v8, /device:TPU:1, one launch (start us, length us, event | category | flops | bytes accessed | tf_op | source)
XLA Modules:
  0.0 69.8 jit_solution(14398255479860196475)
XLA Ops:
  0.6 0.0 copy-start.1
  0.6 0.0 copy-start
  0.7 0.0 copy-start.2
  0.7 67.2 %shard_map.112 = (f32[64,2,256]{2,1,0:T(2,128)}, f32[64,2,256]{2,1,0:T(2,128)}, f32[64,2,256]{2,1,0:T(2,128)}) custom-call(bf16[4096,256]{1,0:T(8,128)(2,1)} %emb_h.1, s32[2,4096]{1,0:T(2,128)} %sign_h.1, s32[2,4096]{1,0:T(2,128)} %perm_h.1, f32[2,4096]{1,0:T(2,128)} %gauss_h.1, f32[2,4096]{1,0:T(2,128)} %scale_h.1, f32[2,4096]{1,0:T(2,128)} %phase_h.1, ...), custom_call_target="tpu_custom_call" | custom-call | tf_op jit(solution)/shard_map/pallas_call | solution.py:496
  67.9 0.0 copy-done.1
  67.9 0.0 copy-done
  67.9 0.0 copy-done.2
  67.9 1.8 %multiply_add_fusion = (f32[16,8,256]{2,1,0:T(8,128)}, f32[16,8,256]{2,1,0:T(8,128)}, f32[16,8,256]{2,1,0:T(8,128)}) fusion(f32[16,8,256]{2,1,0:T(8,128)} %bitcast.17, f32[16,8,256]{2,1,0:T(8,128)S(1)} %bitcast.10, f32[16,8,256]{2,1,0:T(8,128)S(1)} %bitcast.9, f32[16,8,256]{2,1,0:T(8,128)} %bitcast.16, f32[16,8,256]{2,1,0:T(8,128)} %bitcast.15, ...), kind=kLoop, calls=%fused_computation | loop fusion | flops 196608 | bytes 1179648 | tf_op jit(solution)/shard_map/add | solution.py:561
Async XLA Ops:
  0.6 67.3 %copy-start.1 = (f32[64,2,256]{2,1,0:T(2,128)S(1)}, f32[64,2,256]{2,1,0:T(2,128)}, u32[]{:S(2)}) copy-start(f32[64,2,256]{2,1,0:T(2,128)} %dire_h.1) | copy-start | bytes 393220
  0.6 67.3 %copy-start = (f32[64,2,256]{2,1,0:T(2,128)S(1)}, f32[64,2,256]{2,1,0:T(2,128)}, u32[]{:S(2)}) copy-start(f32[64,2,256]{2,1,0:T(2,128)} %res_h.1) | copy-start | bytes 393220
  0.7 67.3 %copy-start.2 = (f32[64,2,256]{2,1,0:T(2,128)S(1)}, f32[64,2,256]{2,1,0:T(2,128)}, u32[]{:S(2)}) copy-start(f32[64,2,256]{2,1,0:T(2,128)} %param.15) | copy-start | bytes 393220
